TPU v7x, 32 devices: a whole 2x2x4 slice. The times are simulated.
32 devices in a mesh: rep: 2 (over y), dev: 4 (over z), tp: 4 (over x, core).
Axes of the slice: x: 2, y: 2, z: 4, core: 2. Of those that a mesh axis runs over, the one named last changes fastest.
Arguments:
- queries: bfloat16 [192, 8192], P(('rep', 'dev'), 'tp'), parts along dimension 0, may hold values from -5 to 5
- cache_keys: bfloat16 [192, 192, 512], P(('rep', 'dev'), None, 'tp'), parts along dimension 0, may hold values from -5 to 5
- cache_values: bfloat16 [192, 192, 512], P(('rep', 'dev'), None, 'tp'), parts along dimension 0, may hold values from -6 to 6
- new_keys: bfloat16 [192, 512], P(('rep', 'dev'), 'tp'), parts along dimension 0, may hold values from -5 to 5
- new_values: bfloat16 [192, 512], P(('rep', 'dev'), 'tp'), parts along dimension 0, may hold values from -12 to 12
- lengths: int32 [192], P(('rep', 'dev')), parts along dimension 0, may hold values from 1 to 192, 4608 in all
- out_proj: bfloat16 [8192, 4096], P('tp', 'dev'), may hold values from -0.0625 to 0.0625
- residual: bfloat16 [192, 4096], P('rep', 'dev'), parts along dimension 0, may hold values from -8 to 8
- norm_gain: float32 [4096], replicated, may hold values from 0.1 to 1.9
- routes: int32 [192, 8], P('rep'), parts along dimension 0, may hold values from 0 to 31, all different within a row; in each aligned block of 96 rows (0 to 95, 96 to 191, ...) at most 48 rows name the same one
- route_weights: float32 [192, 8], P('rep'), parts along dimension 0, may hold values from 0.1 to 0.6
- gate_weights: bfloat16 [32, 4096, 1536], P('dev', None, 'tp'), may hold values from -0.09375 to 0.09375
- up_weights: bfloat16 [32, 4096, 1536], P('dev', None, 'tp'), may hold values from -0.09375 to 0.09375
- down_weights: bfloat16 [32, 1536, 4096], P('dev', 'tp'), may hold values from -0.15625 to 0.15625
Outputs:
- layer_out: bfloat16 [192, 4096], P('rep', 'dev'), parts along dimension 0
There are 2 independent parts, one for each index of `rep`. A program takes and returns all parts, laid end to end along the dimension named above; an argument that names none is the same for every part. Nothing has to cross between parts.
Inputs may be any that keep to these rules, and one draw needn't show every extreme that they name: `lengths`: some row uses all 192 cached positions. `routes`: each row names 8 different experts; no expert is named by more than 48 rows, a bound that some block reaches.
All inputs are finite; a program needn't handle non-finite values. No bound on the sum of `lengths` on one device may be relied on, other than what follows from the above.
Results may differ from a plain program's by a relative error of at most 0.012.
Values may be sent and summed in bfloat16 or wider, within the bound.
A program may use at most 192 MiB of HBM per device.

v0:
```python
import math

import jax
import jax.numpy as jnp
from jax import lax
from jax.sharding import PartitionSpec as P

HEADS = 64
KV = 4
HEAD = 128
LMAX = 192


EPSILON = 1e-06


def slot_table(routes, expert_count, capacity):
    flat_ids = routes.reshape(-1)
    hit_table = (flat_ids[:, None] == jnp.arange(expert_count, dtype=jnp.int32)[None, :]).astype(
        jnp.int32
    )
    rank_in_expert = jnp.sum(jnp.cumsum(hit_table, axis=0) * hit_table, axis=1) - 1
    slot_index = flat_ids * capacity + rank_in_expert
    owners = jnp.arange(flat_ids.shape[0], dtype=jnp.int32) // routes.shape[1]
    slot_owner = jnp.full((expert_count * capacity,), -1, jnp.int32).at[slot_index].set(owners)
    return (slot_index, slot_owner)


def attend_local(queries, cache_keys, cache_values, new_keys, new_values, lengths):
    row_count = queries.shape[0]
    kv_local = new_keys.shape[1] // HEAD
    group_size = HEADS // KV
    query_part = queries.reshape(row_count, kv_local, group_size, HEAD)
    key_part = cache_keys.reshape(row_count, LMAX, kv_local, HEAD)
    value_part = cache_values.reshape(row_count, LMAX, kv_local, HEAD)
    own_key = new_keys.reshape(row_count, kv_local, HEAD)
    own_value = new_values.reshape(row_count, kv_local, HEAD)
    score_scale = 1.0 / math.sqrt(HEAD)
    scores = (
        jnp.einsum("rkgd,rlkd->rkgl", query_part, key_part, preferred_element_type=jnp.float32)
        * score_scale
    )
    own_score = (
        jnp.einsum("rkgd,rkd->rkg", query_part, own_key, preferred_element_type=jnp.float32)
        * score_scale
    )
    valid_mask = jnp.arange(LMAX, dtype=jnp.int32)[None, :] < lengths[:, None]
    scores = jnp.where(valid_mask[:, None, None, :], scores, -jnp.inf)
    highest = jnp.maximum(jnp.max(scores, axis=-1), own_score)
    exp_scores = jnp.exp(scores - highest[..., None])
    own_exp = jnp.exp(own_score - highest)
    denominator = jnp.sum(exp_scores, axis=-1) + own_exp
    weights = (exp_scores / denominator[..., None]).astype(jnp.bfloat16)
    own_weight = (own_exp / denominator).astype(jnp.bfloat16)
    combined = jnp.einsum(
        "rkgl,rlkd->rkgd", weights, value_part, preferred_element_type=jnp.float32
    )
    combined = (
        combined
        + own_weight.astype(jnp.float32)[..., None] * own_value.astype(jnp.float32)[:, :, None, :]
    )
    return combined.reshape(row_count, -1).astype(jnp.bfloat16)


def on_device(
    queries,
    cache_keys,
    cache_values,
    new_keys,
    new_values,
    lengths,
    out_proj,
    residual,
    norm_gain,
    routes,
    route_weights,
    gate_weights,
    up_weights,
    down_weights,
):
    attended = attend_local(queries, cache_keys, cache_values, new_keys, new_values, lengths)
    projected = jnp.dot(
        lax.all_gather(attended, "dev", axis=0, tiled=True),
        out_proj,
        preferred_element_type=jnp.float32,
    )
    dev_count = lax.axis_size("dev")
    local_width = residual.shape[1]
    summed = lax.psum(projected, "tp")
    mixed_full = residual.astype(jnp.float32) + summed
    sent_rows = mixed_full.astype(jnp.bfloat16)
    experts_here = gate_weights.shape[0]
    expert_count = experts_here * dev_count
    row_total = routes.shape[0]
    top_count = routes.shape[1]
    capacity = 2 * row_total * top_count // expert_count
    send_width = sent_rows.shape[1]
    slot_index, slot_owner = slot_table(routes, expert_count, capacity)
    safe_owner = jnp.maximum(slot_owner, 0)
    outgoing = jnp.where(
        slot_owner[:, None] >= 0, sent_rows[safe_owner], jnp.zeros((), jnp.bfloat16)
    )
    outgoing = outgoing.reshape(expert_count, capacity, send_width)
    values = lax.all_to_all(outgoing, "dev", split_axis=0, concat_axis=2, tiled=True).astype(
        jnp.float32
    )
    mean_square = jnp.mean(values * values, axis=-1, keepdims=True)
    normed = (values * lax.rsqrt(mean_square + EPSILON) * norm_gain).astype(jnp.bfloat16)
    gate_value = jnp.einsum(
        "end,edf->enf", normed, gate_weights, preferred_element_type=jnp.float32
    )
    up_value = jnp.einsum("end,edf->enf", normed, up_weights, preferred_element_type=jnp.float32)
    hidden = (jax.nn.silu(gate_value) * up_value).astype(jnp.bfloat16)
    produced = jnp.einsum(
        "enf,efd->end", hidden, down_weights, preferred_element_type=jnp.float32
    ).astype(jnp.bfloat16)
    returned = lax.all_to_all(produced, "dev", split_axis=2, concat_axis=0, tiled=True)
    picked = returned.reshape(expert_count * capacity, local_width)[slot_index]
    picked = picked.reshape(row_total, top_count, local_width).astype(jnp.float32)
    moe_part = jnp.sum(picked * route_weights[:, :, None], axis=1)
    moe_total = lax.psum(moe_part, "tp")
    return (mixed_full + moe_total).astype(jnp.bfloat16)


def solution(mesh):
    in_specs = (
        P(("rep", "dev"), "tp"),
        P(("rep", "dev"), None, "tp"),
        P(("rep", "dev"), None, "tp"),
        P(("rep", "dev"), "tp"),
        P(("rep", "dev"), "tp"),
        P(("rep", "dev")),
        P("tp", "dev"),
        P("rep", "dev"),
        P(),
        P("rep", None),
        P("rep", None),
        P("dev", None, "tp"),
        P("dev", None, "tp"),
        P("dev", "tp", None),
    )
    out_specs = P("rep", "dev")
    return jax.shard_map(
        on_device, mesh=mesh, in_specs=in_specs, out_specs=out_specs, check_vma=False
    )
```

profile of v0, /device:TPU:0, one launch (start us, length us, event | category | flops | bytes accessed | tf_op | source)
XLA Modules:
  0.0 368.0 jit_solution(16595199454888824388)
XLA Ops:
  6.5 0.0 copy-start
  6.5 0.0 all-reduce.3.cloned.1.call-start
  6.5 0.0 copy-start.2
  6.5 0.9 iota_compare_fusion.2
  7.4 1.1 convert_element_type.72
  8.5 0.9 copy.44
  9.5 0.8 fusion.18
  10.3 0.0 copy-done
  10.3 0.8 fusion.29
  11.1 0.2 fusion.10
  11.4 0.0 copy-start.6
  11.4 0.0 copy-start.4
  11.4 1.8 fusion.3
  13.2 16.2 %all_gather.3 = bf16[96,2048]{1,0:T(8,128)(2,1)S(1)} all-gather(bf16[24,2048]{1,0:T(8,128)(2,1)S(1)} %bitcast.60), channel_id=1, replica_groups=mesh['rep'=2,'dev'=4,'tp'=4] {'dev'}, dimensions={0}, use_global_device_ids=true | all-gather | bytes 491520 | tf_op jit(solution)/shard_map/all_gather | solution.py:83
  29.5 0.0 copy-done.2
  29.5 1.5 fusion.30
  31.0 0.0 all-reduce.3.cloned.1.call-update
  31.1 0.0 copy-done.6
  31.1 0.1 copy.34
  31.2 0.1 eq.29
  31.3 0.1 eq.25
  31.4 0.1 copy.33
  31.5 0.1 mul.93
  31.6 1.7 reduce-window.6
  33.3 0.3 slice_reduce_fusion
  33.6 0.1 fusion.16
  33.7 3.4 scatter_custom_fusion
  37.2 0.1 broadcast_in_dim.49
  37.3 28.3 %all-reduce.3.cloned.1.call-done = f32[96,1024]{1,0:T(8,128)} async-done(((f32[96,1024]{1,0:T(8,128)}), f32[96,1024]{1,0:T(8,128)}) %all-reduce.3.cloned.1.call-update) | async-done | bytes 393232 | tf_op jit(solution)/shard_map/psum | solution.py:89
  65.6 0.0 copy-done.4
  65.6 1.0 fusion.12
  66.6 5.8 %gather_fusion = bf16[1536,1024]{1,0:T(8,128)(2,1)} fusion(bf16[96,1024]{1,0:T(8,128)(2,1)S(1)} %fusion.12, s32[2048]{0:T(1024)S(1)} %pad_clamp_fusion), kind=kCustom, calls=%fused_computation | custom fusion | bytes 6297600 | tf_op jit(solution)/shard_map/gather | solution.py:101
  72.5 2.1 broadcast_select_fusion
  74.5 74.0 %all_to_all.24 = bf16[32,48,1024]{2,1,0:T(8,128)(2,1)S(1)} all-to-all(bf16[32,48,1024]{2,1,0:T(8,128)(2,1)S(1)} %broadcast_select_fusion), channel_id=1, replica_groups=mesh['rep'=2,'dev'=4,'tp'=4] {'dev'}, dimensions={0} | all-to-all | bytes 6291456 | tf_op jit(solution)/shard_map/all_to_all | solution.py:104
  148.5 0.7 multiply_reduce_fusion
  149.2 5.7 %copy.51 = f32[4,8,48,1024]{3,0,2,1:T(4,128)} copy(bf16[4,8,48,1024]{3,2,1,0:T(8,128)(2,1)S(1)} %bitcast.55) | data formatting | bytes 9437184 | tf_op jit(solution)/shard_map/convert_element_type | solution.py:104
  154.9 0.0 copy-start.5
  154.9 8.5 %reshape.170 = f32[8,48,4096]{2,1,0:T(8,128)} reshape(f32[8,48,4,1024]{3,2,1,0:T(4,128)} %bitcast.56) | data formatting | bytes 12582912 | tf_op jit(solution)/shard_map/convert_element_type | solution.py:104
  163.4 0.0 copy-done.5
  163.4 13.5 %fusion.4 = f32[8,48,384]{2,1,0:T(8,128)S(1)} fusion(bf16[8,4096,384]{2,1,0:T(8,128)(2,1)} %param.25, f32[8,48,4096]{2,1,0:T(8,128)} %reshape.170, f32[4096]{0:T(1024)S(1)} %copy-done.5, f32[8,48]{1,0:T(8,128)S(1)} %add_rsqrt_fusion), kind=kOutput, calls=%fused_computation.16 | convolution fusion | flops 1212678144 | bytes 32065024 | tf_op jit(solution)/shard_map/end,edf->enf/dot_general | solution.py:109
  176.9 24.2 %convolution_convert_fusion = bf16[8,48,4096]{2,1,0:T(8,128)(2,1)} fusion(bf16[8,384,4096]{2,1,0:T(8,128)(2,1)} %param.27, bf16[8,4096,384]{2,1,0:T(8,128)(2,1)} %param.26, f32[8,48,4096]{2,1,0:T(8,128)} %reshape.170, f32[4096]{0:T(1024)S(1)} %copy-done.5, f32[8,48]{1,0:T(8,128)S(1)} %add_rsqrt_fusion, f32[8,48,384]{2,1,0:T(8,128)S(1)} %fusion.4), kind=kOutput, calls=%fused_computation.6 | convolution fusion | flops 2423095296 | bytes 60376576 | tf_op jit(solution)/shard_map/enf,efd->end/dot_general | solution.py:114
  201.1 9.7 %copy.38 = bf16[8,48,4096]{1,0,2:T(8,128)(2,1)} copy(bf16[8,48,4096]{2,1,0:T(8,128)(2,1)} %convolution_convert_fusion) | data formatting | bytes 6291456 | tf_op jit(solution)/shard_map/convert_element_type | solution.py:116
  210.8 14.8 %reshape.204 = bf16[4,2,196608]{2,1,0:T(2,128)(2,1)} reshape(bf16[4096,8,48]{2,1,0:T(8,128)(2,1)} %bitcast.53) | data formatting | bytes 6291456
  225.6 0.0 copy-start.7
  225.6 4.8 %all-to-all-start.1 = ((bf16[4,2,196608]{2,1,0:T(2,128)(2,1)}), bf16[4,2,196608]{2,1,0:T(2,128)(2,1)}, u32[]{:S(2)}, u32[]{:S(2)}) async-start(bf16[4,2,196608]{2,1,0:T(2,128)(2,1)} %reshape.204), calls=%async_computation.1 | async-start | bytes 6291456 | tf_op jit(solution)/shard_map/all_to_all | solution.py:117
  230.4 0.0 all-reduce.5.cloned.1.call-start
  230.4 0.0 copy-done.7
  230.5 0.1 copy.40
  230.6 69.6 %all-to-all-done.1 = bf16[4,2,196608]{2,1,0:T(2,128)(2,1)} async-done(((bf16[4,2,196608]{2,1,0:T(2,128)(2,1)}), bf16[4,2,196608]{2,1,0:T(2,128)(2,1)}, u32[]{:S(2)}, u32[]{:S(2)}) %all-to-all-start.1) | async-done | bytes 3145760 | tf_op jit(solution)/shard_map/all_to_all | solution.py:117
  300.2 10.3 %reshape.205 = bf16[4096,8,48]{2,1,0:T(8,128)(2,1)} reshape(bf16[4,2,196608]{2,1,0:T(2,128)(2,1)} %all-to-all-done.1) | data formatting | bytes 6291456
  310.4 9.5 %copy.39 = bf16[8,48,4,1024]{3,1,0,2:T(8,128)(2,1)} copy(bf16[8,48,4,1024]{1,0,3,2:T(8,128)(2,1)} %bitcast.54) | data formatting | bytes 6291456 | tf_op jit(solution)/shard_map/all_to_all | solution.py:117
  320.0 0.0 copy-start.3
  320.0 0.0 copy-start.1
  320.0 6.2 %gather_fusion.1 = bf16[768,1024]{1,0:T(8,128)(2,1)S(1)} fusion(bf16[1536,1024]{1,0:T(8,128)(2,1)} %bitcast.52, s32[1024]{0:T(1024)S(1)} %pad_clamp_fusion.1), kind=kCustom, calls=%fused_computation.1 | custom fusion | bytes 3148800 | tf_op jit(solution)/shard_map/gather | solution.py:118
  326.2 1.7 fusion
  327.9 0.0 all-reduce.5.cloned.1.call-update
  328.0 31.5 %all-reduce.5.cloned.1.call-done = f32[96,1024]{1,0:T(8,128)} async-done(((f32[96,1024]{1,0:T(8,128)}), f32[96,1024]{1,0:T(8,128)}) %all-reduce.5.cloned.1.call-update) | async-done | bytes 393232 | tf_op jit(solution)/shard_map/psum | solution.py:121
  359.4 0.0 copy-done.3
  359.4 1.7 add_convert_fusion
  361.2 0.0 copy-done.1
  (15 shorter events, 0.2 us)
Async XLA Ops:
  6.5 3.8 %copy-start = (bf16[24,192,128]{2,1,0:T(8,128)(2,1)S(1)}, bf16[24,192,128]{2,1,0:T(8,128)(2,1)}, u32[]{:S(2)}) copy-start(bf16[24,192,128]{2,1,0:T(8,128)(2,1)} %param.15) | copy-start | bytes 3538948
  6.5 59.0 %all-reduce.3.cloned.1.call-start = ((), (), s32[]{:S(2)}) async-start(), calls=%async_computation.2 | async-start | bytes 786432 | tf_op jit(solution)/shard_map/psum | solution.py:89
  6.5 22.9 %copy-start.2 = (bf16[2048,1024]{1,0:T(8,128)(2,1)S(1)}, bf16[2048,1024]{1,0:T(8,128)(2,1)}, u32[]{:S(2)}) copy-start(bf16[2048,1024]{1,0:T(8,128)(2,1)} %param.20) | copy-start | bytes 12582916
  11.4 19.7 %copy-start.6 = (s32[96,8]{0,1:T(8,128)S(1)}, s32[96,8]{0,1:T(8,128)}, u32[]{:S(2)}) copy-start(s32[96,8]{0,1:T(8,128)} %param.23) | copy-start | bytes 9220
  11.4 54.2 %copy-start.4 = (bf16[96,1024]{1,0:T(8,128)(2,1)S(1)}, bf16[96,1024]{1,0:T(8,128)(2,1)}, u32[]{:S(2)}) copy-start(bf16[96,1024]{1,0:T(8,128)(2,1)} %param.21) | copy-start | bytes 589828
  154.9 8.5 %copy-start.5 = (f32[4096]{0:T(1024)S(1)}, f32[4096]{0:T(1024)}, u32[]{:S(2)}) copy-start(f32[4096]{0:T(1024)} %param.22) | copy-start | bytes 49156
  225.6 4.9 %copy-start.7 = (f32[96,8]{0,1:T(8,128)S(1)}, f32[96,8]{0,1:T(8,128)}, u32[]{:S(2)}) copy-start(f32[96,8]{0,1:T(8,128)} %param.24) | copy-start | bytes 9220
  225.6 74.6 %all-to-all-start.1 = ((bf16[4,2,196608]{2,1,0:T(2,128)(2,1)}), bf16[4,2,196608]{2,1,0:T(2,128)(2,1)}, u32[]{:S(2)}, u32[]{:S(2)}) async-start(bf16[4,2,196608]{2,1,0:T(2,128)(2,1)} %reshape.204), calls=%async_computation.1 | async-start | bytes 6291456 | tf_op jit(solution)/shard_map/all_to_all | solution.py:117
  230.4 129.0 %all-reduce.5.cloned.1.call-start = ((), (), s32[]{:S(2)}) async-start(), calls=%async_computation.3 | async-start | bytes 786432 | tf_op jit(solution)/shard_map/psum | solution.py:121
  320.0 39.5 %copy-start.3 = (f32[96,1024]{1,0:T(8,128)S(1)}, f32[96,1024]{1,0:T(8,128)}, u32[]{:S(2)}) copy-start(f32[96,1024]{1,0:T(8,128)} %all-reduce.3.cloned.1.call-done) | copy-start | bytes 1179652
  320.0 41.2 %copy-start.1 = (bf16[24,192,128]{2,1,0:T(8,128)(2,1)S(1)}, bf16[24,192,128]{2,1,0:T(8,128)(2,1)}, u32[]{:S(2)}) copy-start(bf16[24,192,128]{2,1,0:T(8,128)(2,1)} %param.15) | copy-start | bytes 3538948
Sparse Core Ops, SparseCore 0:
  31.2 34.3 all-reduce.2
  328.1 31.2 all-reduce.4
where the time goes:
time: 369 us; the launch traced here: 368 us
  waiting for transfers between devices  129 us (35%)
  blocking collectives  90.2 us (24%)
  local copies, waits for them, and re-layouts  75.8 us (21%)
  matrix products  42.7 us (12%)
  between operations  13.6 us (4%)
  other arithmetic  11.5 us (3%)
  starting transfers between devices  4.87 us (1%)
    all_to_all x1, blocking collectives, on_device(): lax.all_to_all(outgoing, 'dev', split_axis=0, concat_axis=2, tiled=True)  74 us
    all_to_all x1, waiting for transfers between devices, on_device(): lax.all_to_all(produced, 'dev', split_axis=2, concat_axis=0, tiled=True)  69.6 us
    psum x1, waiting for transfers between devices, on_device(): moe_total = lax.psum(moe_part, 'tp')  31.5 us
    psum x1, waiting for transfers between devices, on_device(): summed = lax.psum(projected, 'tp')  28.3 us
    unnamed x22, local copies, waits for them, and re-layouts  26.2 us
    dot_general x1, matrix products, on_device(): jnp.einsum('enf,efd->end', hidden, down_weights, preferred_element_type=j...  24.2 us
    all_gather x1, blocking collectives, on_device(): lax.all_gather(attended, 'dev', axis=0, tiled=True)  16.2 us
    convert_element_type x2, local copies, waits for them, and re-layouts, on_device(): lax.all_to_all(outgoing, 'dev', split_axis=0, concat_axis=2, tiled=True)  14.2 us
  transfers between devices with their start and end apart: 3, of which 3 were waited for; matrix products, arithmetic and copies ran while one was open for 2% of the time, Pallas kernels for 0%

commit v1 on v0

--- a/solution.py
+++ b/solution.py
@@ -12,18 +12,6 @@
 
 
 EPSILON = 1e-06
-
-
-def slot_table(routes, expert_count, capacity):
-    flat_ids = routes.reshape(-1)
-    hit_table = (flat_ids[:, None] == jnp.arange(expert_count, dtype=jnp.int32)[None, :]).astype(
-        jnp.int32
-    )
-    rank_in_expert = jnp.sum(jnp.cumsum(hit_table, axis=0) * hit_table, axis=1) - 1
-    slot_index = flat_ids * capacity + rank_in_expert
-    owners = jnp.arange(flat_ids.shape[0], dtype=jnp.int32) // routes.shape[1]
-    slot_owner = jnp.full((expert_count * capacity,), -1, jnp.int32).at[slot_index].set(owners)
-    return (slot_index, slot_owner)
 
 
 def attend_local(queries, cache_keys, cache_values, new_keys, new_values, lengths):
@@ -62,6 +50,22 @@
     return combined.reshape(row_count, -1).astype(jnp.bfloat16)
 
 
+def expert_hidden(sent_rows, norm_gain, routes, route_weights, gate_weights, up_weights):
+    experts_here = gate_weights.shape[0]
+    values = sent_rows.astype(jnp.float32)
+    mean_square = jnp.mean(values * values, axis=-1, keepdims=True)
+    normed = (values * lax.rsqrt(mean_square + EPSILON) * norm_gain).astype(jnp.bfloat16)
+    first = lax.axis_index("dev") * experts_here
+    ids = first + jnp.arange(experts_here, dtype=jnp.int32)
+    hit = routes[:, :, None] == ids[None, None, :]
+    dense = jnp.sum(jnp.where(hit, route_weights[:, :, None], 0.0), axis=1)
+    gate_value = jnp.einsum("nd,edf->enf", normed, gate_weights, preferred_element_type=jnp.float32)
+    up_value = jnp.einsum("nd,edf->enf", normed, up_weights, preferred_element_type=jnp.float32)
+    hidden = jax.nn.silu(gate_value) * up_value * dense.T[:, :, None]
+    hidden = hidden.astype(jnp.bfloat16)
+    return jnp.transpose(hidden, (1, 0, 2)).reshape(hidden.shape[1], -1)
+
+
 def on_device(
     queries,
     cache_keys,
@@ -84,40 +88,13 @@
         out_proj,
         preferred_element_type=jnp.float32,
     )
-    dev_count = lax.axis_size("dev")
-    local_width = residual.shape[1]
     summed = lax.psum(projected, "tp")
     mixed_full = residual.astype(jnp.float32) + summed
-    sent_rows = mixed_full.astype(jnp.bfloat16)
-    experts_here = gate_weights.shape[0]
-    expert_count = experts_here * dev_count
-    row_total = routes.shape[0]
-    top_count = routes.shape[1]
-    capacity = 2 * row_total * top_count // expert_count
-    send_width = sent_rows.shape[1]
-    slot_index, slot_owner = slot_table(routes, expert_count, capacity)
-    safe_owner = jnp.maximum(slot_owner, 0)
-    outgoing = jnp.where(
-        slot_owner[:, None] >= 0, sent_rows[safe_owner], jnp.zeros((), jnp.bfloat16)
-    )
-    outgoing = outgoing.reshape(expert_count, capacity, send_width)
-    values = lax.all_to_all(outgoing, "dev", split_axis=0, concat_axis=2, tiled=True).astype(
-        jnp.float32
-    )
-    mean_square = jnp.mean(values * values, axis=-1, keepdims=True)
-    normed = (values * lax.rsqrt(mean_square + EPSILON) * norm_gain).astype(jnp.bfloat16)
-    gate_value = jnp.einsum(
-        "end,edf->enf", normed, gate_weights, preferred_element_type=jnp.float32
-    )
-    up_value = jnp.einsum("end,edf->enf", normed, up_weights, preferred_element_type=jnp.float32)
-    hidden = (jax.nn.silu(gate_value) * up_value).astype(jnp.bfloat16)
-    produced = jnp.einsum(
-        "enf,efd->end", hidden, down_weights, preferred_element_type=jnp.float32
-    ).astype(jnp.bfloat16)
-    returned = lax.all_to_all(produced, "dev", split_axis=2, concat_axis=0, tiled=True)
-    picked = returned.reshape(expert_count * capacity, local_width)[slot_index]
-    picked = picked.reshape(row_total, top_count, local_width).astype(jnp.float32)
-    moe_part = jnp.sum(picked * route_weights[:, :, None], axis=1)
+    sent_rows = lax.all_gather(mixed_full.astype(jnp.bfloat16), "dev", axis=1, tiled=True)
+    hidden = expert_hidden(sent_rows, norm_gain, routes, route_weights, gate_weights, up_weights)
+    down_flat = down_weights.reshape(-1, down_weights.shape[2])
+    moe_part = jnp.dot(hidden, down_flat, preferred_element_type=jnp.float32)
+    moe_part = lax.psum_scatter(moe_part, "dev", scatter_dimension=1, tiled=True)
     moe_total = lax.psum(moe_part, "tp")
     return (mixed_full + moe_total).astype(jnp.bfloat16)
 

time: 369 us -> 192 us (0.52)
  local copies, waits for them, and re-layouts: 75.8 us -> 0.97 us
  blocking collectives: 90.2 us -> 35.7 us
  waiting for transfers between devices: 129 us -> 102 us
  matrix products: 42.7 us -> 34.8 us
  other arithmetic: 11.5 us -> 4.95 us
  starting transfers between devices: 4.87 us -> 0.09 us
    all_to_all x1 -> x0, blocking collectives: 74 us -> none  [on_device(): lax.all_to_all(outgoing, 'dev', split_axis=0, concat_axis=2, tiled=True)]
    all_to_all x1 -> x0, waiting for transfers between devices: 69.6 us -> none  [on_device(): lax.all_to_all(produced, 'dev', split_axis=2, concat_axis=0, tiled=True)]
    reduce_scatter x0 -> x1, waiting for transfers between devices: none -> 33.9 us  [on_device(): lax.psum_scatter(moe_part, 'dev', scatter_dimension=1, tiled=True)]
    unnamed x22 -> x20, local copies, waits for them, and re-layouts: 26.2 us -> 0.97 us
    convert_element_type x3 -> x0, local copies, waits for them, and re-layouts: 23.9 us -> none  [the longest x2 14.2 us: on_device(): lax.all_to_all(outgoing, 'dev', split_axis=0, concat_axis=2, tiled=True)]
    all_gather x0 -> x1, blocking collectives: none -> 19.5 us  [on_device(): lax.all_gather(mixed_full.astype(jnp.bfloat16), 'dev', axis=1, tiled=True)]
    gather x2 -> x0, local copies, waits for them, and re-layouts: 12.1 us -> none  [the longest x1 6.23 us: on_device(): picked = returned.reshape(expert_count * capacity, local_width)[slot_index]]
    all_to_all x1 -> x0, local copies, waits for them, and re-layouts: 9.54 us -> none  [on_device(): lax.all_to_all(produced, 'dev', split_axis=2, concat_axis=0, tiled=True)]
  transfers between devices with their start and end apart: 3 -> 3, of which waited for: 3 -> 3; matrix products, arithmetic and copies ran while one was open for 2% -> 0% of each run, Pallas kernels for 0% -> 0%
where the time goes in v1:
time: 192 us
  waiting for transfers between devices  102 us (53%)
  blocking collectives  35.7 us (19%)
  matrix products  34.8 us (18%)
  between operations  13.2 us (7%)
  other arithmetic  4.95 us (3%)
    psum x1, waiting for transfers between devices, on_device(): summed = lax.psum(projected, 'tp')  34.3 us
    psum x1, waiting for transfers between devices, on_device(): moe_total = lax.psum(moe_part, 'tp')  34 us
    reduce_scatter x1, waiting for transfers between devices, on_device(): lax.psum_scatter(moe_part, 'dev', scatter_dimension=1, tiled=True)  33.9 us
    dot_general x1, matrix products, on_device(): moe_part = jnp.dot(hidden, down_flat, preferred_element_type=jnp.float32)  20.8 us
    all_gather x1, blocking collectives, on_device(): lax.all_gather(mixed_full.astype(jnp.bfloat16), 'dev', axis=1, tiled=True)  19.5 us
    all_gather x1, blocking collectives, on_device(): lax.all_gather(attended, 'dev', axis=0, tiled=True)  16.2 us
    dot_general x1, matrix products, expert_hidden(): jnp.einsum('nd,edf->enf', normed, gate_weights, preferred_element_type=jn...  10.4 us
  transfers between devices with their start and end apart: 3, of which 3 were waited for; matrix products, arithmetic and copies ran while one was open for 0% of the time, Pallas kernels for 0%

profile of v1, /device:TPU:0, one launch (start us, length us, event | category | flops | bytes accessed | tf_op | source)
XLA Modules:
  0.0 192.1 jit_solution(188442647359878207)
XLA Ops:
  6.5 0.0 copy-start
  6.5 0.0 copy-start.8
  6.5 0.0 all-reduce.3.cloned.1.call-start
  6.5 0.9 iota_compare_fusion
  7.4 0.7 convert_element_type.45
  8.1 0.9 copy.19
  9.0 0.8 fusion.23
  9.9 0.0 copy-done
  9.9 0.0 copy-start.2
  9.9 0.8 fusion.28
  10.7 0.2 fusion.19
  11.0 0.0 copy-done.8
  11.0 0.5 fusion.11
  11.5 16.2 %all_gather.6 = bf16[96,2048]{1,0:T(8,128)(2,1)S(1)} all-gather(bf16[24,2048]{1,0:T(8,128)(2,1)S(1)} %bitcast.27), channel_id=1, replica_groups=mesh['rep'=2,'dev'=4,'tp'=4] {'dev'}, dimensions={0}, use_global_device_ids=true | all-gather | bytes 491520 | tf_op jit(solution)/shard_map/all_gather | solution.py:87
  27.7 0.0 copy-done.2
  27.7 0.0 copy-start.6
  27.7 0.0 copy-start.7
  27.7 0.0 copy-start.5
  27.7 1.5 fusion.29
  29.3 0.0 copy-start.4
  29.3 0.0 all-reduce.3.cloned.1.call-update
  29.3 0.0 reduce-scatter.2.cloned.1.call-start
  29.4 0.0 copy-done.6
  29.4 0.0 copy-done.7
  29.4 0.1 select_reduce_fusion
  29.5 34.3 %all-reduce.3.cloned.1.call-done = f32[96,1024]{1,0:T(8,128)} async-done(((f32[96,1024]{1,0:T(8,128)}), f32[96,1024]{1,0:T(8,128)}) %all-reduce.3.cloned.1.call-update) | async-done | bytes 393232 | tf_op jit(solution)/shard_map/psum | solution.py:91
  63.8 0.0 copy-done.5
  63.8 1.0 fusion.20
  64.8 19.5 %all_gather.7 = bf16[96,4096]{1,0:T(8,128)(2,1)S(1)} all-gather(bf16[96,1024]{1,0:T(8,128)(2,1)S(1)} %fusion.20), channel_id=1, replica_groups=mesh['rep'=2,'dev'=4,'tp'=4] {'dev'}, dimensions={1}, use_global_device_ids=true | all-gather | bytes 983040 | tf_op jit(solution)/shard_map/all_gather | solution.py:93
  84.3 0.3 fusion
  84.6 0.0 copy-done.4
  84.6 10.4 %fusion.17 = f32[96,8,384]{2,0,1:T(8,128)S(1)} fusion(bf16[8,4096,384]{2,1,0:T(8,128)(2,1)} %param.25, bf16[96,4096]{1,0:T(8,128)(2,1)S(1)} %all_gather.7, f32[4096]{0:T(1024)S(1)} %copy-done.4, f32[96]{0:T(128)S(1)} %add_rsqrt_fusion), kind=kOutput, calls=%fused_computation.21 | convolution fusion | flops 2417491968 | bytes 27148672 | tf_op jit(solution)/shard_map/nd,edf->enf/dot_general | solution.py:62
  95.0 20.8 %convolution_bitcast_fusion = f32[96,4096]{1,0:T(8,128)} fusion(bf16[8,384,4096]{2,1,0:T(8,128)(2,1)} %param.27, bf16[8,4096,384]{2,1,0:T(8,128)(2,1)} %param.26, f32[96,8,384]{2,0,1:T(8,128)S(1)} %fusion.17, f32[96,8]{0,1:T(8,128)S(1)} %select_reduce_fusion, bf16[96,4096]{1,0:T(8,128)(2,1)S(1)} %all_gather.7, f32[4096]{0:T(1024)S(1)} %copy-done.4, ...), kind=kOutput, calls=%fused_computation | convolution fusion | flops 4835475456 | bytes 53890432 | tf_op jit(solution)/shard_map/dot_general | solution.py:96
  115.8 0.0 copy-start.3
  115.8 0.0 copy-start.1
  115.8 0.0 reduce-scatter.2.cloned.1.call-update
  115.8 0.0 all-reduce.5.cloned.1.call-start
  115.8 33.9 %reduce-scatter.2.cloned.1.call-done = f32[96,1024]{1,0:T(8,128)} async-done(((f32[96,4096]{1,0:T(8,128)}), f32[96,1024]{1,0:T(8,128)}) %reduce-scatter.2.cloned.1.call-update) | async-done | bytes 393232 | tf_op jit(solution)/shard_map/reduce_scatter | solution.py:97
  149.8 0.0 all-reduce.5.cloned.1.call-update
  149.8 34.0 %all-reduce.5.cloned.1.call-done = f32[96,1024]{1,0:T(8,128)} async-done(((f32[96,1024]{1,0:T(8,128)}), f32[96,1024]{1,0:T(8,128)}) %all-reduce.5.cloned.1.call-update) | async-done | bytes 393232 | tf_op jit(solution)/shard_map/psum | solution.py:98
  183.8 0.0 copy-done.3
  183.8 1.7 add_convert_fusion
  185.6 0.0 copy-done.1
  (5 shorter events, 0.1 us)
Async XLA Ops:
  6.5 3.3 %copy-start = (bf16[24,192,128]{2,1,0:T(8,128)(2,1)S(1)}, bf16[24,192,128]{2,1,0:T(8,128)(2,1)}, u32[]{:S(2)}) copy-start(bf16[24,192,128]{2,1,0:T(8,128)(2,1)} %param.15) | copy-start | bytes 3538948
  6.5 4.4 %copy-start.8 = (bf16[24,192,128]{2,1,0:T(8,128)(2,1)S(1)}, bf16[24,192,128]{2,1,0:T(8,128)(2,1)}, u32[]{:S(2)}) copy-start(bf16[24,192,128]{2,1,0:T(8,128)(2,1)} %param.16) | copy-start | bytes 3538948
  6.5 57.3 %all-reduce.3.cloned.1.call-start = ((), (), s32[]{:S(2)}) async-start(), calls=%async_computation.1 | async-start | bytes 786432 | tf_op jit(solution)/shard_map/psum | solution.py:91
  9.9 17.9 %copy-start.2 = (bf16[2048,1024]{1,0:T(8,128)(2,1)S(1)}, bf16[2048,1024]{1,0:T(8,128)(2,1)}, u32[]{:S(2)}) copy-start(bf16[2048,1024]{1,0:T(8,128)(2,1)} %param.20) | copy-start | bytes 12582916
  27.7 1.6 copy-start.6
  27.7 1.7 copy-start.7
  27.7 36.1 %copy-start.5 = (bf16[96,1024]{1,0:T(8,128)(2,1)S(1)}, bf16[96,1024]{1,0:T(8,128)(2,1)}, u32[]{:S(2)}) copy-start(bf16[96,1024]{1,0:T(8,128)(2,1)} %param.21) | copy-start | bytes 589828
  29.3 55.3 %copy-start.4 = (f32[4096]{0:T(1024)S(1)}, f32[4096]{0:T(1024)}, u32[]{:S(2)}) copy-start(f32[4096]{0:T(1024)} %param.22) | copy-start | bytes 49156
  29.3 120.5 %reduce-scatter.2.cloned.1.call-start = ((), (), s32[]{:S(2)}) async-start(), calls=%async_computation.2 | async-start | bytes 1966080 | tf_op jit(solution)/shard_map/reduce_scatter | solution.py:97
  115.8 68.1 %copy-start.3 = (f32[96,1024]{1,0:T(8,128)S(1)}, f32[96,1024]{1,0:T(8,128)}, u32[]{:S(2)}) copy-start(f32[96,1024]{1,0:T(8,128)} %all-reduce.3.cloned.1.call-done) | copy-start | bytes 1179652
  115.8 69.8 %copy-start.1 = (bf16[24,192,128]{2,1,0:T(8,128)(2,1)S(1)}, bf16[24,192,128]{2,1,0:T(8,128)(2,1)}, u32[]{:S(2)}) copy-start(bf16[24,192,128]{2,1,0:T(8,128)(2,1)} %param.15) | copy-start | bytes 3538948
  115.8 68.0 %all-reduce.5.cloned.1.call-start = ((), (), s32[]{:S(2)}) async-start(), calls=%async_computation.3 | async-start | bytes 786432 | tf_op jit(solution)/shard_map/psum | solution.py:98
Sparse Core Ops, SparseCore 0:
  29.4 34.3 all-reduce.2
  115.9 33.8 reduce-scatter.1
  152.2 31.5 all-reduce.4

commit v2 on v1

--- a/solution.py
+++ b/solution.py
@@ -1,8 +1,11 @@
+import functools
 import math
 
 import jax
 import jax.numpy as jnp
 from jax import lax
+from jax.experimental import pallas as pl
+from jax.experimental.pallas import tpu as pltpu
 from jax.sharding import PartitionSpec as P
 
 HEADS = 64
@@ -50,11 +53,237 @@
     return combined.reshape(row_count, -1).astype(jnp.bfloat16)
 
 
-def expert_hidden(sent_rows, norm_gain, routes, route_weights, gate_weights, up_weights):
+MESH = pl.DeviceIdType.MESH
+VMEM_BYTES = 58 * 1024 * 1024
+
+
+def places(dev_count):
+    me, t = lax.axis_index("dev"), lax.axis_index("tp")
+    par, half = t % 2, t // 2
+    return me, t, par, half, t + 1 - 2 * par, t + 2 - 4 * half
+
+
+def greet(me, dev_count, near, far):
+    barrier = pltpu.get_barrier_semaphore()
+    for k in range(1, dev_count):
+        pl.semaphore_signal(
+            barrier, inc=1, device_id={"dev": lax.rem(me + k, dev_count)}, device_id_type=MESH
+        )
+    pl.semaphore_signal(barrier, inc=1, device_id={"tp": near}, device_id_type=MESH)
+    pl.semaphore_signal(barrier, inc=1, device_id={"tp": far}, device_id_type=MESH)
+    pl.semaphore_wait(barrier, dev_count + 1)
+
+
+def send(src, dst, send_sem, recv_sem, where):
+    copy = pltpu.make_async_remote_copy(
+        src_ref=src, dst_ref=dst, send_sem=send_sem, recv_sem=recv_sem, device_id=where,
+        device_id_type=MESH,
+    )
+    copy.start()
+    return copy
+
+
+def sum_over_tp(acc, out1, in1, out2, in2, sems, par, half, near, far):
+    out1[...] = acc[1 - par].astype(jnp.bfloat16)
+    first = send(out1, in1, sems.at[0], sems.at[1], {"tp": near})
+    first.wait_recv()
+    out2[...] = (acc[par, 1 - half] + in1[1 - half].astype(jnp.float32)).astype(jnp.bfloat16)
+    second = send(out2, in2, sems.at[2], sems.at[3], {"tp": far})
+    kept = acc[par, half] + in1[half].astype(jnp.float32)
+    second.wait_recv()
+    first.wait_send()
+    second.wait_send()
+    return kept + in2[...].astype(jnp.float32)
+
+
+def project_kernel(
+    dev_count, attended, out_proj, residual, gain, normed, mixed,
+    gathered, weights, acc, rest, out1, in1, out2, in2, rows_all, wide,
+    load_sem, ag_send, ag_recv, tp_sems, z_send, z_recv, x_send, x_recv, c_sems,
+):
+    me, t, par, half, near, far = places(dev_count)
+    greet(me, dev_count, near, far)
+    load = pltpu.make_async_copy(out_proj, weights, load_sem)
+    load.start()
+    copies = []
+    for k in range(1, dev_count):
+        copies.append(send(
+            attended, gathered.at[me], ag_send.at[k], ag_recv.at[k],
+            {"dev": lax.rem(me + k, dev_count)},
+        ))
+    gathered[me] = attended[...]
+    rows, width = rest.shape[1], rest.shape[2]
+    total = dev_count * attended.shape[0]
+    rest[...] = residual[...].astype(jnp.float32).reshape(rest.shape)
+    load.wait()
+    for copy in copies:
+        copy.wait()
+    features = gathered[...].astype(jnp.float32).reshape(total, -1).astype(jnp.bfloat16)
+    projected = jnp.dot(features, weights[...], preferred_element_type=jnp.float32)
+    projected = projected.reshape(2, 2, rows, width)
+    for h in range(2):
+        for p in range(2):
+            acc[p, h] = projected[h, p]
+    block = rest[t] + sum_over_tp(
+        acc, out1, in1, out2, in2, tp_sems, par, half, near, far
+    )
+    mixed[...] = block
+    rows_all[par, half, me] = block.astype(jnp.bfloat16)
+    across = []
+    for k in range(1, dev_count):
+        across.append(send(
+            rows_all.at[par, half, me], rows_all.at[par, half, me], z_send.at[k], z_recv.at[k],
+            {"dev": lax.rem(me + k, dev_count)},
+        ))
+    over = [send(
+        rows_all.at[par, half, me], rows_all.at[par, half, me], x_send.at[0], x_recv.at[0],
+        {"tp": far},
+    )]
+    for k in range(1, dev_count):
+        across[k - 1].wait_recv()
+        source = lax.rem(me - k + dev_count, dev_count)
+        over.append(send(
+            rows_all.at[par, half, source], rows_all.at[par, half, source],
+            x_send.at[k], x_recv.at[k], {"tp": far},
+        ))
+    mine = send(
+        rows_all.at[par, half], rows_all.at[par, half], c_sems.at[0], c_sems.at[1], {"tp": near}
+    )
+    for copy in over:
+        copy.wait_recv()
+    theirs = send(
+        rows_all.at[par, 1 - half], rows_all.at[par, 1 - half], c_sems.at[2], c_sems.at[3],
+        {"tp": near},
+    )
+    mine.wait_recv()
+    theirs.wait_recv()
+    for h in range(2):
+        for p in range(2):
+            values = jnp.concatenate(
+                [rows_all[p, h, d].astype(jnp.float32) for d in range(dev_count)], axis=1
+            )
+            mean_square = jnp.mean(values * values, axis=-1, keepdims=True)
+            first = (2 * h + p) * rows
+            wide[first:first + rows, :] = values * lax.rsqrt(mean_square + EPSILON) * gain[...]
+    normed[...] = wide[...].astype(jnp.bfloat16)
+    for copy in across:
+        copy.wait_send()
+    for copy in over:
+        copy.wait_send()
+    mine.wait_send()
+    theirs.wait_send()
+
+
+def project(attended, out_proj, residual, norm_gain, tp_count):
+    total, width = residual.shape
+    dev_count = total // attended.shape[0]
+    rows = total // tp_count
+    bf16, f32 = jnp.bfloat16, jnp.float32
+    vmem = pl.BlockSpec(memory_space=pltpu.VMEM)
+    dma = pltpu.SemaphoreType.DMA
+    return pl.pallas_call(
+        functools.partial(project_kernel, dev_count),
+        out_shape=(
+            jax.ShapeDtypeStruct((total, dev_count * width), bf16),
+            jax.ShapeDtypeStruct((rows, width), f32),
+        ),
+        in_specs=[vmem, pl.BlockSpec(memory_space=pl.ANY), vmem, vmem],
+        out_specs=(vmem, vmem),
+        scratch_shapes=[
+            pltpu.VMEM((dev_count,) + attended.shape, bf16),
+            pltpu.VMEM(out_proj.shape, bf16),
+            pltpu.VMEM((2, 2, rows, width), f32),
+            pltpu.VMEM((4, rows, width), f32),
+            pltpu.VMEM((2, rows, width), bf16),
+            pltpu.VMEM((2, rows, width), bf16),
+            pltpu.VMEM((rows, width), bf16),
+            pltpu.VMEM((rows, width), bf16),
+            pltpu.VMEM((2, 2, dev_count, rows, width), bf16),
+            pltpu.VMEM((total, dev_count * width), f32),
+            dma, dma((dev_count,)), dma((dev_count,)), dma((4,)),
+            dma((dev_count,)), dma((dev_count,)), dma((dev_count,)), dma((dev_count,)), dma((4,)),
+        ],
+        compiler_params=pltpu.CompilerParams(
+            collective_id=0, has_side_effects=True, vmem_limit_bytes=VMEM_BYTES
+        ),
+    )(attended, out_proj, residual, norm_gain.reshape(1, -1))
+
+
+def finish_kernel(
+    dev_count, partial, mixed, layer_out,
+    acc, out1, in1, out2, in2, chunks, out3, in3, done,
+    tp_sems, z_send, z_recv, g_sems,
+):
+    me, t, par, half, near, far = places(dev_count)
+    greet(me, dev_count, near, far)
+    rows, width = mixed.shape
+    for h in range(2):
+        for p in range(2):
+            first = (2 * h + p) * rows
+            acc[p, h] = partial[first:first + rows, :]
+    summed = sum_over_tp(
+        acc, out1, in1, out2, in2, tp_sems, par, half, near, far
+    )
+    for d in range(dev_count):
+        chunk = summed[:, d * width:(d + 1) * width]
+        chunks[d] = chunk
+        out3[d] = chunk.astype(jnp.bfloat16)
+    copies = []
+    for k in range(1, dev_count):
+        peer = lax.rem(me + k, dev_count)
+        copies.append(send(
+            out3.at[peer], in3.at[me], z_send.at[k], z_recv.at[k], {"dev": peer}
+        ))
+    block = mixed[...] + chunks[me]
+    for k in range(1, dev_count):
+        copies[k - 1].wait_recv()
+        block = block + in3[lax.rem(me - k + dev_count, dev_count)].astype(jnp.float32)
+    done[par, half] = block.astype(jnp.bfloat16)
+    over = send(
+        done.at[par, half], done.at[par, half], g_sems.at[0], g_sems.at[1], {"tp": far}
+    )
+    over.wait()
+    both = send(done.at[par], done.at[par], g_sems.at[2], g_sems.at[3], {"tp": near})
+    both.wait()
+    whole = jnp.concatenate(
+        [done[p, h].astype(jnp.float32) for h in range(2) for p in range(2)], axis=0
+    )
+    layer_out[...] = whole.astype(jnp.bfloat16)
+    for copy in copies:
+        copy.wait_send()
+
+
+def finish(partial, mixed, dev_count):
+    rows, width = mixed.shape
+    total, full = partial.shape
+    bf16, f32 = jnp.bfloat16, jnp.float32
+    vmem = pl.BlockSpec(memory_space=pltpu.VMEM)
+    dma = pltpu.SemaphoreType.DMA
+    return pl.pallas_call(
+        functools.partial(finish_kernel, dev_count),
+        out_shape=jax.ShapeDtypeStruct((total, width), bf16),
+        in_specs=[vmem, vmem],
+        out_specs=vmem,
+        scratch_shapes=[
+            pltpu.VMEM((2, 2, rows, full), f32),
+            pltpu.VMEM((2, rows, full), bf16),
+            pltpu.VMEM((2, rows, full), bf16),
+            pltpu.VMEM((rows, full), bf16),
+            pltpu.VMEM((rows, full), bf16),
+            pltpu.VMEM((dev_count, rows, width), f32),
+            pltpu.VMEM((dev_count, rows, width), bf16),
+            pltpu.VMEM((dev_count, rows, width), bf16),
+            pltpu.VMEM((2, 2, rows, width), bf16),
+            dma((4,)), dma((dev_count,)), dma((dev_count,)), dma((4,)),
+        ],
+        compiler_params=pltpu.CompilerParams(
+            collective_id=1, has_side_effects=True, vmem_limit_bytes=VMEM_BYTES
+        ),
+    )(partial, mixed)
+
+
+def expert_hidden(normed, routes, route_weights, gate_weights, up_weights):
     experts_here = gate_weights.shape[0]
-    values = sent_rows.astype(jnp.float32)
-    mean_square = jnp.mean(values * values, axis=-1, keepdims=True)
-    normed = (values * lax.rsqrt(mean_square + EPSILON) * norm_gain).astype(jnp.bfloat16)
     first = lax.axis_index("dev") * experts_here
     ids = first + jnp.arange(experts_here, dtype=jnp.int32)
     hit = routes[:, :, None] == ids[None, None, :]
@@ -83,20 +312,11 @@
     down_weights,
 ):
     attended = attend_local(queries, cache_keys, cache_values, new_keys, new_values, lengths)
-    projected = jnp.dot(
-        lax.all_gather(attended, "dev", axis=0, tiled=True),
-        out_proj,
-        preferred_element_type=jnp.float32,
-    )
-    summed = lax.psum(projected, "tp")
-    mixed_full = residual.astype(jnp.float32) + summed
-    sent_rows = lax.all_gather(mixed_full.astype(jnp.bfloat16), "dev", axis=1, tiled=True)
-    hidden = expert_hidden(sent_rows, norm_gain, routes, route_weights, gate_weights, up_weights)
+    normed, mixed = project(attended, out_proj, residual, norm_gain, lax.axis_size("tp"))
+    hidden = expert_hidden(normed, routes, route_weights, gate_weights, up_weights)
     down_flat = down_weights.reshape(-1, down_weights.shape[2])
     moe_part = jnp.dot(hidden, down_flat, preferred_element_type=jnp.float32)
-    moe_part = lax.psum_scatter(moe_part, "dev", scatter_dimension=1, tiled=True)
-    moe_total = lax.psum(moe_part, "tp")
-    return (mixed_full + moe_total).astype(jnp.bfloat16)
+    return finish(moe_part, mixed, lax.axis_size("dev"))
 
 
 def solution(mesh):

time: 192 us -> 92.9 us (0.48)
  waiting for transfers between devices: 102 us -> 0 us
  Pallas kernels: 0 us -> 53.1 us
  blocking collectives: 35.7 us -> 0 us
  between operations: 13.2 us -> 0.1 us
  other arithmetic: 4.95 us -> 2.57 us
  local copies, waits for them, and re-layouts: 0.97 us -> 3.22 us
    psum x2 -> x0, waiting for transfers between devices: 68.4 us -> none  [the longest x1 34.3 us: on_device(): summed = lax.psum(projected, 'tp')]
    pallas_call x0 -> x2, Pallas kernels: none -> 53.1 us  [the longest x1 31.2 us: project(): pl.pallas_call(functools.partial(project_kernel, dev_count), out_shape=(j...]
    all_gather x2 -> x0, blocking collectives: 35.7 us -> none  [the longest x1 19.5 us: on_device(): lax.all_gather(mixed_full.astype(jnp.bfloat16), 'dev', axis=1, tiled=True)]
    reduce_scatter x1 -> x0, waiting for transfers between devices: 33.9 us -> none  [on_device(): lax.psum_scatter(moe_part, 'dev', scatter_dimension=1, tiled=True)]
    convert_element_type x2 -> x0, other arithmetic: 2.76 us -> none  [the longest x1 1.73 us: on_device(): return (mixed_full + moe_total).astype(jnp.bfloat16)]
    unnamed x20 -> x11, local copies, waits for them, and re-layouts: 0.97 us -> 3.22 us
  transfers between devices with their start and end apart: 3 -> 0, of which waited for: 3 -> 0; matrix products, arithmetic and copies ran while one was open for 0% -> 0% of each run, Pallas kernels for 0% -> 0%
where the time goes in v2:
time: 92.9 us; the launch traced here: 92.6 us
  Pallas kernels  53.1 us (57%)
  matrix products  33.6 us (36%)
  local copies, waits for them, and re-layouts  3.22 us (3%)
  other arithmetic  2.57 us (3%)
    pallas_call x1, Pallas kernels, project(): pl.pallas_call(functools.partial(project_kernel, dev_count), out_shape=(j...  31.2 us
    pallas_call x1, Pallas kernels, finish(): pl.pallas_call(functools.partial(finish_kernel, dev_count), out_shape=jax...  21.9 us
    dot_general x1, matrix products, on_device(): moe_part = jnp.dot(hidden, down_flat, preferred_element_type=jnp.float32)  20.8 us
    dot_general x1, matrix products, expert_hidden(): jnp.einsum('nd,edf->enf', normed, gate_weights, preferred_element_type=jn...  10.6 us
    unnamed x11, local copies, waits for them, and re-layouts  3.22 us

profile of v2, /device:TPU:0, one launch (start us, length us, event | category | flops | bytes accessed | tf_op | source)
XLA Modules:
  0.0 92.6 jit_solution(4269211238770772642)
XLA Ops:
  0.0 0.0 copy-start
  0.0 0.9 select_reduce_fusion
  0.9 0.7 iota_compare_fusion
  1.6 0.7 convert_element_type.28
  2.3 0.9 copy.19
  3.2 0.0 copy-start.3
  3.2 0.9 %fusion.18 = f32[24,1,16]{2,1,0:T(1,128)S(1)} fusion(bf16[24,16,128]{2,1,0:T(8,128)(2,1)S(1)} %bitcast.25, bf16[24,128,1]{1,0,2:T(8,128)(2,1)} %bitcast.33), kind=kOutput, calls=%fused_computation.26 | convolution fusion | flops 98304 | bytes 105984 | tf_op jit(solution)/shard_map/rkgd,rkd->rkg/dot_general | solution.py:35
  4.2 0.0 copy-done
  4.2 0.8 fusion.23
  5.0 0.2 fusion.15
  5.3 0.0 copy-done.3
  5.3 0.5 fusion.8
  5.8 0.7 copy.24
  6.4 31.2 %shard_map.136 = (bf16[96,4096]{1,0:T(8,128)(2,1)}, f32[24,1024]{1,0:T(8,128)}) custom-call(bf16[24,2048]{1,0:T(8,128)(2,1)} %bitcast.27, bf16[2048,1024]{1,0:T(8,128)(2,1)} %out_proj.1, bf16[96,1024]{1,0:T(8,128)(2,1)} %residual.1, f32[1,4096]{1,0:T(1,128)} %bitcast.32), custom_call_target="tpu_custom_call" | custom-call | tf_op jit(solution)/shard_map/pallas_call | solution.py:184
  37.7 0.0 copy-start.2
  37.7 10.6 %fusion.11 = f32[96,8,384]{2,0,1:T(8,128)S(1)} fusion(bf16[8,4096,384]{2,1,0:T(8,128)(2,1)} %param.25, bf16[96,4096]{1,0:T(8,128)(2,1)} %get-tuple-element.7), kind=kOutput, calls=%fused_computation.14 | convolution fusion | flops 2415919104 | bytes 27131904 | tf_op jit(solution)/shard_map/nd,edf->enf/dot_general | solution.py:291
  48.3 0.0 copy-done.2
  48.3 0.0 copy-start.1
  48.3 20.8 %convolution_bitcast_fusion.partial = f32[96,4096]{1,0:T(8,128)} fusion(bf16[8,384,4096]{2,1,0:T(8,128)(2,1)} %param.27, bf16[8,4096,384]{2,1,0:T(8,128)(2,1)} %param.26, f32[96,8,384]{2,0,1:T(8,128)S(1)} %fusion.11, bf16[96,4096]{1,0:T(8,128)(2,1)S(1)} %copy-done.2, f32[96,8]{0,1:T(8,128)S(1)} %select_reduce_fusion), kind=kOutput, calls=%fused_computation | convolution fusion | flops 4833902592 | bytes 53873664 | tf_op jit(solution)/shard_map/dot_general | solution.py:318
  69.1 21.9 %shard_map.137 = bf16[96,1024]{1,0:T(8,128)(2,1)} custom-call(f32[96,4096]{1,0:T(8,128)} %convolution_bitcast_fusion.partial, f32[24,1024]{1,0:T(8,128)} %get-tuple-element.8.mixed), custom_call_target="tpu_custom_call" | custom-call | tf_op jit(solution)/shard_map/pallas_call | solution.py:262
  91.0 1.6 %copy.26 = bf16[96,1024]{1,0:T(8,128)(2,1)} copy(bf16[96,1024]{1,0:T(8,128)(2,1)} %shard_map.137) | data formatting | bytes 393216
  92.6 0.0 copy-done.1
  (3 shorter events, 0.0 us)
Async XLA Ops:
  0.0 4.2 %copy-start = (bf16[24,192,128]{2,1,0:T(8,128)(2,1)S(1)}, bf16[24,192,128]{2,1,0:T(8,128)(2,1)}, u32[]{:S(2)}) copy-start(bf16[24,192,128]{2,1,0:T(8,128)(2,1)} %param.15) | copy-start | bytes 3538948
  3.2 2.0 %copy-start.3 = (bf16[24,192,128]{2,1,0:T(8,128)(2,1)S(1)}, bf16[24,192,128]{2,1,0:T(8,128)(2,1)}, u32[]{:S(2)}) copy-start(bf16[24,192,128]{2,1,0:T(8,128)(2,1)} %param.16) | copy-start | bytes 3538948
  37.7 10.6 %copy-start.2 = (bf16[96,4096]{1,0:T(8,128)(2,1)S(1)}, bf16[96,4096]{1,0:T(8,128)(2,1)}, u32[]{:S(2)}) copy-start(bf16[96,4096]{1,0:T(8,128)(2,1)} %get-tuple-element.7) | copy-start | bytes 2359300
  48.3 44.3 %copy-start.1 = (bf16[24,192,128]{2,1,0:T(8,128)(2,1)S(1)}, bf16[24,192,128]{2,1,0:T(8,128)(2,1)}, u32[]{:S(2)}) copy-start(bf16[24,192,128]{2,1,0:T(8,128)(2,1)} %param.15) | copy-start | bytes 3538948

commit v3 on v2

v3 whole, which is shorter than its diff:
```python
import functools
import math

import jax
import jax.numpy as jnp
from jax import lax
from jax.experimental import pallas as pl
from jax.experimental.pallas import tpu as pltpu
from jax.sharding import PartitionSpec as P

HEADS = 64
KV = 4
HEAD = 128
LMAX = 192


EPSILON = 1e-06


def attend_local(queries, cache_keys, cache_values, new_keys, new_values, lengths):
    row_count = queries.shape[0]
    kv_local = new_keys.shape[1] // HEAD
    group_size = HEADS // KV
    query_part = queries.reshape(row_count, kv_local, group_size, HEAD)
    key_part = cache_keys.reshape(row_count, LMAX, kv_local, HEAD)
    value_part = cache_values.reshape(row_count, LMAX, kv_local, HEAD)
    own_key = new_keys.reshape(row_count, kv_local, HEAD)
    own_value = new_values.reshape(row_count, kv_local, HEAD)
    score_scale = 1.0 / math.sqrt(HEAD)
    scores = (
        jnp.einsum("rkgd,rlkd->rkgl", query_part, key_part, preferred_element_type=jnp.float32)
        * score_scale
    )
    own_score = (
        jnp.einsum("rkgd,rkd->rkg", query_part, own_key, preferred_element_type=jnp.float32)
        * score_scale
    )
    valid_mask = jnp.arange(LMAX, dtype=jnp.int32)[None, :] < lengths[:, None]
    scores = jnp.where(valid_mask[:, None, None, :], scores, -jnp.inf)
    highest = jnp.maximum(jnp.max(scores, axis=-1), own_score)
    exp_scores = jnp.exp(scores - highest[..., None])
    own_exp = jnp.exp(own_score - highest)
    denominator = jnp.sum(exp_scores, axis=-1) + own_exp
    weights = (exp_scores / denominator[..., None]).astype(jnp.bfloat16)
    own_weight = (own_exp / denominator).astype(jnp.bfloat16)
    combined = jnp.einsum(
        "rkgl,rlkd->rkgd", weights, value_part, preferred_element_type=jnp.float32
    )
    combined = (
        combined
        + own_weight.astype(jnp.float32)[..., None] * own_value.astype(jnp.float32)[:, :, None, :]
    )
    return combined.reshape(row_count, -1).astype(jnp.bfloat16)


MESH = pl.DeviceIdType.MESH
VMEM_BYTES = 60 * 1024 * 1024


def places(dev_count):
    me, t = lax.axis_index("dev"), lax.axis_index("tp")
    par, half = t % 2, t // 2
    return me, t, par, half, t + 1 - 2 * par, t + 2 - 4 * half


def greet(me, dev_count, near, far):
    barrier = pltpu.get_barrier_semaphore()
    for k in range(1, dev_count):
        pl.semaphore_signal(
            barrier, inc=1, device_id={"dev": lax.rem(me + k, dev_count)}, device_id_type=MESH
        )
    pl.semaphore_signal(barrier, inc=1, device_id={"tp": near}, device_id_type=MESH)
    pl.semaphore_signal(barrier, inc=1, device_id={"tp": far}, device_id_type=MESH)
    pl.semaphore_wait(barrier, dev_count + 1)


def send(src, dst, send_sem, recv_sem, where):
    copy = pltpu.make_async_remote_copy(
        src_ref=src, dst_ref=dst, send_sem=send_sem, recv_sem=recv_sem, device_id=where,
        device_id_type=MESH,
    )
    copy.start()
    return copy


def sum_over_tp(acc, rows, out1, in1, out2, in2, sems, par, half, near, far):
    def block(h, p):
        return acc[pl.ds(pl.multiple_of((2 * h + p) * rows, 8), rows), :]

    for h in range(2):
        out1[h] = block(h, 1 - par).astype(jnp.bfloat16)
    first = send(out1, in1, sems.at[0], sems.at[1], {"tp": near})
    first.wait_recv()
    out2[...] = (block(1 - half, par) + in1[1 - half].astype(jnp.float32)).astype(jnp.bfloat16)
    second = send(out2, in2, sems.at[2], sems.at[3], {"tp": far})
    kept = block(half, par) + in1[half].astype(jnp.float32)
    second.wait_recv()
    first.wait_send()
    second.wait_send()
    return kept + in2[...].astype(jnp.float32)


def layer_kernel(
    dev_count, attended, out_proj, residual, gain, dense, gate, up, down, layer_out,
    gathered, weights, acc, rest, out1, in1, out2, in2, rows_all, mixed, normed,
    units, downs, hidden, wide, big_out1, big_in1, big_out2, big_in2, chunks, out3, in3, done,
    load_sem, ag_send, ag_recv, tp_sems, z_send, z_recv, x_send, x_recv, c_sems,
    gate_sem, up_sem, down_sem, big_sems, r_send, r_recv, g_sems,
):
    bf16, f32 = jnp.bfloat16, jnp.float32
    me, t, par, half, near, far = places(dev_count)
    experts, ff = gate.shape[0], gate.shape[2]
    groups, slots, down_slots = down.shape[0], units.shape[0], downs.shape[0]

    def unit_loads(e):
        slot = lax.rem(e, slots)
        return (
            pltpu.make_async_copy(gate.at[e], units.at[slot, :, 0:ff], gate_sem.at[slot]),
            pltpu.make_async_copy(up.at[e], units.at[slot, :, ff:2 * ff], up_sem.at[slot]),
        )

    def down_load(g):
        slot = lax.rem(g, down_slots)
        return pltpu.make_async_copy(down.at[g], downs.at[slot], down_sem.at[slot])

    greet(me, dev_count, near, far)
    copies = []
    for k in range(1, dev_count):
        copies.append(send(
            attended, gathered.at[me], ag_send.at[k], ag_recv.at[k],
            {"dev": lax.rem(me + k, dev_count)},
        ))
    load = pltpu.make_async_copy(out_proj, weights, load_sem)
    load.start()
    for e in range(slots):
        for copy in unit_loads(jnp.int32(e)):
            copy.start()
    for g in range(down_slots):
        down_load(jnp.int32(g)).start()
    gathered[me] = attended[...]
    rows, width = rest.shape[1], rest.shape[2]
    total = dev_count * attended.shape[0]
    rest[...] = residual[...].astype(f32).reshape(rest.shape)
    load.wait()
    for copy in copies:
        copy.wait()
    features = gathered[...].astype(f32).reshape(total, -1).astype(bf16)
    acc[...] = jnp.dot(features, weights[...], preferred_element_type=f32)
    block = rest[t] + sum_over_tp(
        acc, rows, out1, in1, out2, in2, tp_sems, par, half, near, far
    )
    mixed[...] = block
    rows_all[par, half, me] = block.astype(bf16)
    across = []
    for k in range(1, dev_count):
        across.append(send(
            rows_all.at[par, half, me], rows_all.at[par, half, me], z_send.at[k], z_recv.at[k],
            {"dev": lax.rem(me + k, dev_count)},
        ))
    over = [send(
        rows_all.at[par, half, me], rows_all.at[par, half, me], x_send.at[0], x_recv.at[0],
        {"tp": far},
    )]
    for k in range(1, dev_count):
        across[k - 1].wait_recv()
        source = lax.rem(me - k + dev_count, dev_count)
        over.append(send(
            rows_all.at[par, half, source], rows_all.at[par, half, source],
            x_send.at[k], x_recv.at[k], {"tp": far},
        ))
    mine = send(
        rows_all.at[par, half], rows_all.at[par, half], c_sems.at[0], c_sems.at[1], {"tp": near}
    )
    for copy in over:
        copy.wait_recv()
    theirs = send(
        rows_all.at[par, 1 - half], rows_all.at[par, 1 - half], c_sems.at[2], c_sems.at[3],
        {"tp": near},
    )
    mine.wait_recv()
    theirs.wait_recv()
    for h in range(2):
        for p in range(2):
            values = jnp.concatenate(
                [rows_all[p, h, d].astype(f32) for d in range(dev_count)], axis=1
            )
            mean_square = jnp.mean(values * values, axis=-1, keepdims=True)
            first = (2 * h + p) * rows
            wide[first:first + rows, :] = values * lax.rsqrt(mean_square + EPSILON) * gain[...]
    normed[...] = wide[...].astype(bf16)
    wide[...] = jnp.zeros_like(wide)

    def expert_step(e, carry):
        for copy in unit_loads(e):
            copy.wait()
        both = jnp.dot(
            normed[...], units[lax.rem(e, slots)], preferred_element_type=f32
        )
        value = both[:, :ff]
        value = value / (1.0 + jnp.exp(-value)) * both[:, ff:] * dense[e]
        hidden[e] = value.astype(bf16)
        if slots < experts:
            @pl.when(e + slots < experts)
            def _():
                for copy in unit_loads(e + slots):
                    copy.start()
        return carry

    lax.fori_loop(0, experts, expert_step, 0)
    per_group = experts // groups
    step = math.gcd(wide.shape[1], 1024)

    def down_step(g, carry):
        down_load(g).wait()
        slot = lax.rem(g, down_slots)
        inner = jnp.concatenate(
            [hidden[g * per_group + i] for i in range(per_group)], axis=1
        )
        for c in range(0, wide.shape[1], step):
            wide[:, c:c + step] += jnp.dot(
                inner, downs[slot, :, c:c + step], preferred_element_type=f32
            )
        if down_slots < groups:
            @pl.when(g + down_slots < groups)
            def _():
                down_load(g + down_slots).start()
        return carry

    lax.fori_loop(0, groups, down_step, 0)
    summed = sum_over_tp(
        wide, rows, big_out1, big_in1, big_out2, big_in2, big_sems, par, half, near, far
    )
    for d in range(dev_count):
        chunk = summed[:, d * width:(d + 1) * width]
        chunks[d] = chunk
        out3[d] = chunk.astype(bf16)
    returns = []
    for k in range(1, dev_count):
        peer = lax.rem(me + k, dev_count)
        returns.append(send(
            out3.at[peer], in3.at[me], r_send.at[k], r_recv.at[k], {"dev": peer}
        ))
    block = mixed[...] + chunks[me]
    for k in range(1, dev_count):
        returns[k - 1].wait_recv()
        block = block + in3[lax.rem(me - k + dev_count, dev_count)].astype(f32)
    done[par, half] = block.astype(bf16)
    last = send(done.at[par, half], done.at[par, half], g_sems.at[0], g_sems.at[1], {"tp": far})
    last.wait()
    pair = send(done.at[par], done.at[par], g_sems.at[2], g_sems.at[3], {"tp": near})
    pair.wait()
    whole = jnp.concatenate(
        [done[p, h].astype(f32) for h in range(2) for p in range(2)], axis=0
    )
    layer_out[...] = whole.astype(bf16)
    for copy in across + over + [mine, theirs] + returns:
        copy.wait_send()


def layer(attended, out_proj, residual, norm_gain, dense, gate, up, down):
    total, width = residual.shape
    dev_count = total // attended.shape[0]
    rows = total // 4
    full = dev_count * width
    experts, _, ff = gate.shape
    groups = experts // 2 if experts % 2 == 0 else experts
    down = down.reshape(groups, -1, full)
    slots, down_slots = min(5, experts), min(2, groups)
    bf16, f32 = jnp.bfloat16, jnp.float32
    vmem = pl.BlockSpec(memory_space=pltpu.VMEM)
    hbm = pl.BlockSpec(memory_space=pl.ANY)
    dma = pltpu.SemaphoreType.DMA
    per_dev = dma((dev_count,))
    return pl.pallas_call(
        functools.partial(layer_kernel, dev_count),
        out_shape=jax.ShapeDtypeStruct((total, width), bf16),
        in_specs=[vmem, hbm, vmem, vmem, vmem, hbm, hbm, hbm],
        out_specs=vmem,
        scratch_shapes=[
            pltpu.VMEM((dev_count,) + attended.shape, bf16),
            pltpu.VMEM(out_proj.shape, bf16),
            pltpu.VMEM((total, width), f32),
            pltpu.VMEM((4, rows, width), f32),
            pltpu.VMEM((2, rows, width), bf16),
            pltpu.VMEM((2, rows, width), bf16),
            pltpu.VMEM((rows, width), bf16),
            pltpu.VMEM((rows, width), bf16),
            pltpu.VMEM((2, 2, dev_count, rows, width), bf16),
            pltpu.VMEM((rows, width), f32),
            pltpu.VMEM((total, full), bf16),
            pltpu.VMEM((slots, full, 2 * ff), bf16),
            pltpu.VMEM((down_slots,) + down.shape[1:], bf16),
            pltpu.VMEM((experts, total, ff), bf16),
            pltpu.VMEM((total, full), f32),
            pltpu.VMEM((2, rows, full), bf16),
            pltpu.VMEM((2, rows, full), bf16),
            pltpu.VMEM((rows, full), bf16),
            pltpu.VMEM((rows, full), bf16),
            pltpu.VMEM((dev_count, rows, width), f32),
            pltpu.VMEM((dev_count, rows, width), bf16),
            pltpu.VMEM((dev_count, rows, width), bf16),
            pltpu.VMEM((2, 2, rows, width), bf16),
            dma, per_dev, per_dev, dma((4,)), per_dev, per_dev, per_dev, per_dev, dma((4,)),
            dma((slots,)), dma((slots,)), dma((down_slots,)), dma((4,)), per_dev, per_dev,
            dma((4,)),
        ],
        compiler_params=pltpu.CompilerParams(
            collective_id=0, has_side_effects=True, vmem_limit_bytes=VMEM_BYTES
        ),
    )(attended, out_proj, residual, norm_gain.reshape(1, -1), dense, gate, up, down)


def dense_weights(routes, route_weights, experts_here):
    ids = lax.axis_index("dev") * experts_here + jnp.arange(experts_here, dtype=jnp.int32)
    hit = routes[None, :, :] == ids[:, None, None]
    return jnp.sum(jnp.where(hit, route_weights[None], 0.0), axis=2, keepdims=True)


def on_device(
    queries,
    cache_keys,
    cache_values,
    new_keys,
    new_values,
    lengths,
    out_proj,
    residual,
    norm_gain,
    routes,
    route_weights,
    gate_weights,
    up_weights,
    down_weights,
):
    attended = attend_local(queries, cache_keys, cache_values, new_keys, new_values, lengths)
    dense = dense_weights(routes, route_weights, gate_weights.shape[0])
    return layer(
        attended, out_proj, residual, norm_gain, dense, gate_weights, up_weights, down_weights
    )


def solution(mesh):
    in_specs = (
        P(("rep", "dev"), "tp"),
        P(("rep", "dev"), None, "tp"),
        P(("rep", "dev"), None, "tp"),
        P(("rep", "dev"), "tp"),
        P(("rep", "dev"), "tp"),
        P(("rep", "dev")),
        P("tp", "dev"),
        P("rep", "dev"),
        P(),
        P("rep", None),
        P("rep", None),
        P("dev", None, "tp"),
        P("dev", None, "tp"),
        P("dev", "tp", None),
    )
    out_specs = P("rep", "dev")
    return jax.shard_map(
        on_device, mesh=mesh, in_specs=in_specs, out_specs=out_specs, check_vma=False
    )
```

time: 92.9 us -> 76 us (0.82)
  matrix products: 33.6 us -> 2.23 us
  Pallas kernels: 53.1 us -> 66.7 us
  local copies, waits for them, and re-layouts: 3.22 us -> 4.15 us
    dot_general x2 -> x0, matrix products: 31.4 us -> none  [the longest x1 20.8 us: on_device(): moe_part = jnp.dot(hidden, down_flat, preferred_element_type=jnp.float32)]
    pallas_call x2 -> x1, Pallas kernels: 53.1 us -> 66.7 us  [layer(): pl.pallas_call(functools.partial(layer_kernel, dev_count), out_shape=jax....]
    broadcast_in_dim x0 -> x1, local copies, waits for them, and re-layouts: none -> 0.94 us  [dense_weights(): jnp.sum(jnp.where(hit, route_weights[None], 0.0), axis=2, keepdims=True)]
    unnamed x11 -> x9, local copies, waits for them, and re-layouts: 3.22 us -> 3.21 us
where the time goes in v3:
time: 76 us; the launch traced here: 75.8 us
  Pallas kernels  66.7 us (88%)
  local copies, waits for them, and re-layouts  4.15 us (5%)
  other arithmetic  2.58 us (3%)
  matrix products  2.23 us (3%)
    pallas_call x1, Pallas kernels, layer(): pl.pallas_call(functools.partial(layer_kernel, dev_count), out_shape=jax....  66.7 us
    unnamed x9, local copies, waits for them, and re-layouts  3.21 us

profile of v3, /device:TPU:0, one launch (start us, length us, event | category | flops | bytes accessed | tf_op | source)
XLA Modules:
  0.0 75.8 jit_solution(18141716421116081723)
XLA Ops:
  0.0 0.0 copy-start
  0.0 0.9 %select_reduce_fusion = f32[8,96]{1,0:T(8,128)S(1)} fusion(f32[96,8]{0,1:T(8,128)} %param.24, s32[96,8]{0,1:T(8,128)} %param.23, s32[8]{0:T(128)S(1)} %iota_add_fusion), kind=kLoop, calls=%fused_computation.10 | loop fusion | flops 17664 | bytes 9248 | tf_op jit(solution)/shard_map/reduce_sum | solution.py:316
  0.9 0.7 iota_compare_fusion
  1.6 0.7 convert_element_type.24
  2.3 0.9 %copy.23 = bf16[3,8,16,128]{3,2,1,0:T(8,128)(2,1)S(1)} copy(bf16[3,8,16,128]{3,1,2,0:T(8,128)(2,1)} %bitcast.20) | data formatting | bytes 196608
  3.2 0.0 copy-start.2
  3.2 0.9 %fusion.5 = f32[24,1,16]{2,1,0:T(1,128)S(1)} fusion(bf16[24,16,128]{2,1,0:T(8,128)(2,1)S(1)} %bitcast.18, bf16[24,128,1]{1,0,2:T(8,128)(2,1)} %bitcast.26), kind=kOutput, calls=%fused_computation.12 | convolution fusion | flops 98304 | bytes 105984 | tf_op jit(solution)/shard_map/rkgd,rkd->rkg/dot_general | solution.py:35
  4.2 0.0 copy-done
  4.2 0.8 %fusion.9 = (f32[24,16]{1,0:T(8,128)S(1)}, f32[24,16,192]{2,1,0:T(8,128)S(1)}) fusion(bf16[24,16,128]{2,1,0:T(8,128)(2,1)S(1)} %bitcast.19, bf16[24,192,128]{2,1,0:T(8,128)(2,1)S(1)} %copy-done, pred[24,192]{1,0:T(8,128)(4,1)S(1)} %iota_compare_fusion), kind=kOutput, calls=%fused_computation.20 | convolution fusion | flops 19095168 | bytes 1579008 | tf_op jit(solution)/shard_map/rkgd,rlkd->rkgl/dot_general | solution.py:31
  5.0 0.2 fusion.2
  5.3 0.0 copy-done.2
  5.3 0.5 fusion.1
  5.8 0.7 copy.28
  6.4 0.9 %copy.20.dense = f32[8,96,1]{2,1,0:T(8,128)} copy(f32[8,96,1]{1,0,2:T(8,128)S(1)} %bitcast.25) | data formatting | bytes 6144 | tf_op jit(solution)/shard_map/broadcast_in_dim | solution.py:316
  7.4 0.0 copy-start.1
  7.4 66.7 %shard_map.136 = bf16[96,1024]{1,0:T(8,128)(2,1)} custom-call(bf16[24,2048]{1,0:T(8,128)(2,1)} %bitcast.17, bf16[2048,1024]{1,0:T(8,128)(2,1)} %out_proj.1, bf16[96,1024]{1,0:T(8,128)(2,1)} %residual.1, f32[1,4096]{1,0:T(1,128)} %bitcast.24, f32[8,96,1]{2,1,0:T(8,128)} %copy.20.dense, bf16[8,4096,384]{2,1,0:T(8,128)(2,1)} %gate.1, bf16[8,4096,384]{2,1,0:T(8,128)(2,1)} %up.1, ...), custom_call_target="tpu_custom_call" | custom-call | tf_op jit(solution)/shard_map/pallas_call | solution.py:274
  74.1 1.6 %copy.30 = bf16[96,1024]{1,0:T(8,128)(2,1)} copy(bf16[96,1024]{1,0:T(8,128)(2,1)} %shard_map.136) | data formatting | bytes 393216
  75.7 0.0 copy-done.1
  (3 shorter events, 0.0 us)
Async XLA Ops:
  0.0 4.2 %copy-start = (bf16[24,192,128]{2,1,0:T(8,128)(2,1)S(1)}, bf16[24,192,128]{2,1,0:T(8,128)(2,1)}, u32[]{:S(2)}) copy-start(bf16[24,192,128]{2,1,0:T(8,128)(2,1)} %param.15) | copy-start | bytes 3538948
  3.2 2.0 %copy-start.2 = (bf16[24,192,128]{2,1,0:T(8,128)(2,1)S(1)}, bf16[24,192,128]{2,1,0:T(8,128)(2,1)}, u32[]{:S(2)}) copy-start(bf16[24,192,128]{2,1,0:T(8,128)(2,1)} %param.16) | copy-start | bytes 3538948
  7.4 68.4 %copy-start.1 = (bf16[24,192,128]{2,1,0:T(8,128)(2,1)S(1)}, bf16[24,192,128]{2,1,0:T(8,128)(2,1)}, u32[]{:S(2)}) copy-start(bf16[24,192,128]{2,1,0:T(8,128)(2,1)} %param.15) | copy-start | bytes 3538948

commit v4 on v3

--- a/solution.py
+++ b/solution.py
@@ -105,12 +105,13 @@
     gathered, weights, acc, rest, out1, in1, out2, in2, rows_all, mixed, normed,
     units, downs, hidden, wide, big_out1, big_in1, big_out2, big_in2, chunks, out3, in3, done,
     load_sem, ag_send, ag_recv, tp_sems, z_send, z_recv, x_send, x_recv, c_sems,
-    gate_sem, up_sem, down_sem, big_sems, r_send, r_recv, g_sems,
+    gate_sem, up_sem, down_sem, n_send, n_recv, f_send, f_recv, r_send, r_recv, g_sems,
 ):
     bf16, f32 = jnp.bfloat16, jnp.float32
     me, t, par, half, near, far = places(dev_count)
     experts, ff = gate.shape[0], gate.shape[2]
-    groups, slots, down_slots = down.shape[0], units.shape[0], downs.shape[0]
+    slots, down_slots = units.shape[0], downs.shape[0]
+    rows, width = rest.shape[1], rest.shape[2]
 
     def unit_loads(e):
         slot = lax.rem(e, slots)
@@ -119,9 +120,11 @@
             pltpu.make_async_copy(up.at[e], units.at[slot, :, ff:2 * ff], up_sem.at[slot]),
         )
 
-    def down_load(g):
-        slot = lax.rem(g, down_slots)
-        return pltpu.make_async_copy(down.at[g], downs.at[slot], down_sem.at[slot])
+    def down_load(k):
+        first = pl.multiple_of(lax.rem(me + k + 1, dev_count) * width, 128)
+        return pltpu.make_async_copy(
+            down.at[:, pl.ds(first, width)], downs.at[k % down_slots], down_sem.at[k % down_slots]
+        )
 
     greet(me, dev_count, near, far)
     copies = []
@@ -136,9 +139,8 @@
         for copy in unit_loads(jnp.int32(e)):
             copy.start()
     for g in range(down_slots):
-        down_load(jnp.int32(g)).start()
+        down_load(g).start()
     gathered[me] = attended[...]
-    rows, width = rest.shape[1], rest.shape[2]
     total = dev_count * attended.shape[0]
     rest[...] = residual[...].astype(f32).reshape(rest.shape)
     load.wait()
@@ -188,7 +190,6 @@
             first = (2 * h + p) * rows
             wide[first:first + rows, :] = values * lax.rsqrt(mean_square + EPSILON) * gain[...]
     normed[...] = wide[...].astype(bf16)
-    wide[...] = jnp.zeros_like(wide)
 
     def expert_step(e, carry):
         for copy in unit_loads(e):
@@ -207,43 +208,49 @@
         return carry
 
     lax.fori_loop(0, experts, expert_step, 0)
-    per_group = experts // groups
-    step = math.gcd(wide.shape[1], 1024)
-
-    def down_step(g, carry):
-        down_load(g).wait()
-        slot = lax.rem(g, down_slots)
-        inner = jnp.concatenate(
-            [hidden[g * per_group + i] for i in range(per_group)], axis=1
-        )
-        for c in range(0, wide.shape[1], step):
-            wide[:, c:c + step] += jnp.dot(
-                inner, downs[slot, :, c:c + step], preferred_element_type=f32
+    inner = jnp.concatenate([hidden[i] for i in range(experts)], axis=1)
+
+    def rows_of(k, h, p):
+        first = pl.multiple_of((2 * h + p) * rows, 8)
+        return wide[pl.ds(first, rows), k * width:(k + 1) * width]
+
+    nears, fars, returns = [], [], []
+    for k in range(dev_count + 2):
+        if k < dev_count:
+            down_load(k).wait()
+            wide[:, k * width:(k + 1) * width] = jnp.dot(
+                inner, downs[k % down_slots], preferred_element_type=f32
             )
-        if down_slots < groups:
-            @pl.when(g + down_slots < groups)
-            def _():
-                down_load(g + down_slots).start()
-        return carry
-
-    lax.fori_loop(0, groups, down_step, 0)
-    summed = sum_over_tp(
-        wide, rows, big_out1, big_in1, big_out2, big_in2, big_sems, par, half, near, far
-    )
-    for d in range(dev_count):
-        chunk = summed[:, d * width:(d + 1) * width]
-        chunks[d] = chunk
-        out3[d] = chunk.astype(bf16)
-    returns = []
-    for k in range(1, dev_count):
-        peer = lax.rem(me + k, dev_count)
-        returns.append(send(
-            out3.at[peer], in3.at[me], r_send.at[k], r_recv.at[k], {"dev": peer}
-        ))
-    block = mixed[...] + chunks[me]
-    for k in range(1, dev_count):
-        returns[k - 1].wait_recv()
-        block = block + in3[lax.rem(me - k + dev_count, dev_count)].astype(f32)
+            if k + down_slots < dev_count:
+                down_load(k + down_slots).start()
+            for h in range(2):
+                big_out1[k, h] = rows_of(k, h, 1 - par).astype(bf16)
+            nears.append(send(
+                big_out1.at[k], big_in1.at[k], n_send.at[k], n_recv.at[k], {"tp": near}
+            ))
+        if 1 <= k <= dev_count:
+            j = k - 1
+            nears[j].wait_recv()
+            big_out2[j] = (rows_of(j, 1 - half, par) + big_in1[j, 1 - half].astype(f32)).astype(bf16)
+            fars.append(send(
+                big_out2.at[j], big_in2.at[j], f_send.at[j], f_recv.at[j], {"tp": far}
+            ))
+            chunks[j] = rows_of(j, half, par) + big_in1[j, half].astype(f32)
+        if k >= 2:
+            j = k - 2
+            fars[j].wait_recv()
+            chunk = chunks[j] + big_in2[j].astype(f32)
+            if j < dev_count - 1:
+                out3[j] = chunk.astype(bf16)
+                returns.append(send(
+                    out3.at[j], in3.at[j], r_send.at[j], r_recv.at[j],
+                    {"dev": lax.rem(me + j + 1, dev_count)},
+                ))
+            else:
+                block = mixed[...] + chunk
+    for j in range(dev_count - 1):
+        returns[j].wait_recv()
+        block = block + in3[j].astype(f32)
     done[par, half] = block.astype(bf16)
     last = send(done.at[par, half], done.at[par, half], g_sems.at[0], g_sems.at[1], {"tp": far})
     last.wait()
@@ -253,7 +260,7 @@
         [done[p, h].astype(f32) for h in range(2) for p in range(2)], axis=0
     )
     layer_out[...] = whole.astype(bf16)
-    for copy in across + over + [mine, theirs] + returns:
+    for copy in across + over + [mine, theirs] + nears + fars + returns:
         copy.wait_send()
 
 
@@ -263,9 +270,8 @@
     rows = total // 4
     full = dev_count * width
     experts, _, ff = gate.shape
-    groups = experts // 2 if experts % 2 == 0 else experts
-    down = down.reshape(groups, -1, full)
-    slots, down_slots = min(5, experts), min(2, groups)
+    down = down.reshape(-1, full)
+    slots, down_slots = min(5, experts), min(2, dev_count)
     bf16, f32 = jnp.bfloat16, jnp.float32
     vmem = pl.BlockSpec(memory_space=pltpu.VMEM)
     hbm = pl.BlockSpec(memory_space=pl.ANY)
@@ -289,19 +295,20 @@
             pltpu.VMEM((rows, width), f32),
             pltpu.VMEM((total, full), bf16),
             pltpu.VMEM((slots, full, 2 * ff), bf16),
-            pltpu.VMEM((down_slots,) + down.shape[1:], bf16),
+            pltpu.VMEM((down_slots, down.shape[0], width), bf16),
             pltpu.VMEM((experts, total, ff), bf16),
             pltpu.VMEM((total, full), f32),
-            pltpu.VMEM((2, rows, full), bf16),
-            pltpu.VMEM((2, rows, full), bf16),
-            pltpu.VMEM((rows, full), bf16),
-            pltpu.VMEM((rows, full), bf16),
+            pltpu.VMEM((dev_count, 2, rows, width), bf16),
+            pltpu.VMEM((dev_count, 2, rows, width), bf16),
+            pltpu.VMEM((dev_count, rows, width), bf16),
+            pltpu.VMEM((dev_count, rows, width), bf16),
             pltpu.VMEM((dev_count, rows, width), f32),
             pltpu.VMEM((dev_count, rows, width), bf16),
             pltpu.VMEM((dev_count, rows, width), bf16),
             pltpu.VMEM((2, 2, rows, width), bf16),
             dma, per_dev, per_dev, dma((4,)), per_dev, per_dev, per_dev, per_dev, dma((4,)),
-            dma((slots,)), dma((slots,)), dma((down_slots,)), dma((4,)), per_dev, per_dev,
+            dma((slots,)), dma((slots,)), dma((down_slots,)), per_dev, per_dev, per_dev, per_dev,
+            per_dev, per_dev,
             dma((4,)),
         ],
         compiler_params=pltpu.CompilerParams(

time: 76 us -> 70.5 us (0.928)
  Pallas kernels: 66.7 us -> 61.2 us
    pallas_call x1, Pallas kernels: 66.7 us -> 61.2 us  [layer(): pl.pallas_call(functools.partial(layer_kernel, dev_count), out_shape=jax....]
where the time goes in v4:
time: 70.5 us; the launch traced here: 70.2 us
  Pallas kernels  61.2 us (87%)
  local copies, waits for them, and re-layouts  4.15 us (6%)
  other arithmetic  2.58 us (4%)
  matrix products  2.23 us (3%)
    pallas_call x1, Pallas kernels, layer(): pl.pallas_call(functools.partial(layer_kernel, dev_count), out_shape=jax....  61.2 us
    unnamed x9, local copies, waits for them, and re-layouts  3.21 us

profile of v4, /device:TPU:0, one launch (start us, length us, event | category | flops | bytes accessed | tf_op | source)
XLA Modules:
  0.0 70.2 jit_solution(1867133966114782120)
XLA Ops:
  0.0 0.0 copy-start
  0.0 0.9 %select_reduce_fusion = f32[8,96]{1,0:T(8,128)S(1)} fusion(f32[96,8]{0,1:T(8,128)} %param.24, s32[96,8]{0,1:T(8,128)} %param.23, s32[8]{0:T(128)S(1)} %iota_add_fusion), kind=kLoop, calls=%fused_computation.10 | loop fusion | flops 17664 | bytes 9248 | tf_op jit(solution)/shard_map/reduce_sum | solution.py:323
  0.9 0.7 %iota_compare_fusion = pred[24,192]{1,0:T(8,128)(4,1)S(1)} fusion(s32[24]{0:T(128)} %param.19), kind=kLoop, calls=%fused_computation.11 | loop fusion | flops 4608 | bytes 4704 | tf_op jit(solution)/shard_map/lt | solution.py:38
  1.6 0.7 convert_element_type.24
  2.3 0.9 %copy.23 = bf16[3,8,16,128]{3,2,1,0:T(8,128)(2,1)S(1)} copy(bf16[3,8,16,128]{3,1,2,0:T(8,128)(2,1)} %bitcast.20) | data formatting | bytes 196608
  3.2 0.0 copy-start.2
  3.2 0.9 %fusion.5 = f32[24,1,16]{2,1,0:T(1,128)S(1)} fusion(bf16[24,16,128]{2,1,0:T(8,128)(2,1)S(1)} %bitcast.18, bf16[24,128,1]{1,0,2:T(8,128)(2,1)} %bitcast.26), kind=kOutput, calls=%fused_computation.12 | convolution fusion | flops 98304 | bytes 105984 | tf_op jit(solution)/shard_map/rkgd,rkd->rkg/dot_general | solution.py:35
  4.2 0.0 copy-done
  4.2 0.8 %fusion.9 = (f32[24,16]{1,0:T(8,128)S(1)}, f32[24,16,192]{2,1,0:T(8,128)S(1)}) fusion(bf16[24,16,128]{2,1,0:T(8,128)(2,1)S(1)} %bitcast.19, bf16[24,192,128]{2,1,0:T(8,128)(2,1)S(1)} %copy-done, pred[24,192]{1,0:T(8,128)(4,1)S(1)} %iota_compare_fusion), kind=kOutput, calls=%fused_computation.20 | convolution fusion | flops 19095168 | bytes 1579008 | tf_op jit(solution)/shard_map/rkgd,rlkd->rkgl/dot_general | solution.py:31
  5.0 0.2 fusion.2
  5.3 0.0 copy-done.2
  5.3 0.5 fusion.1
  5.8 0.7 copy.28
  6.4 0.9 %copy.20.dense = f32[8,96,1]{2,1,0:T(8,128)} copy(f32[8,96,1]{1,0,2:T(8,128)S(1)} %bitcast.25) | data formatting | bytes 6144 | tf_op jit(solution)/shard_map/broadcast_in_dim | solution.py:323
  7.4 0.0 copy-start.1
  7.4 61.2 %shard_map.136 = bf16[96,1024]{1,0:T(8,128)(2,1)} custom-call(bf16[24,2048]{1,0:T(8,128)(2,1)} %bitcast.17, bf16[2048,1024]{1,0:T(8,128)(2,1)} %out_proj.1, bf16[96,1024]{1,0:T(8,128)(2,1)} %residual.1, f32[1,4096]{1,0:T(1,128)} %bitcast.24, f32[8,96,1]{2,1,0:T(8,128)} %copy.20.dense, bf16[8,4096,384]{2,1,0:T(8,128)(2,1)} %gate.1, bf16[8,4096,384]{2,1,0:T(8,128)(2,1)} %up.1, ...), custom_call_target="tpu_custom_call" | custom-call | tf_op jit(solution)/shard_map/pallas_call | solution.py:280
  68.6 1.6 %copy.30 = bf16[96,1024]{1,0:T(8,128)(2,1)} copy(bf16[96,1024]{1,0:T(8,128)(2,1)} %shard_map.136) | data formatting | bytes 393216
  70.2 0.0 copy-done.1
  (3 shorter events, 0.0 us)
Async XLA Ops:
  0.0 4.2 %copy-start = (bf16[24,192,128]{2,1,0:T(8,128)(2,1)S(1)}, bf16[24,192,128]{2,1,0:T(8,128)(2,1)}, u32[]{:S(2)}) copy-start(bf16[24,192,128]{2,1,0:T(8,128)(2,1)} %param.15) | copy-start | bytes 3538948
  3.2 2.0 %copy-start.2 = (bf16[24,192,128]{2,1,0:T(8,128)(2,1)S(1)}, bf16[24,192,128]{2,1,0:T(8,128)(2,1)}, u32[]{:S(2)}) copy-start(bf16[24,192,128]{2,1,0:T(8,128)(2,1)} %param.16) | copy-start | bytes 3538948
  7.4 62.8 %copy-start.1 = (bf16[24,192,128]{2,1,0:T(8,128)(2,1)S(1)}, bf16[24,192,128]{2,1,0:T(8,128)(2,1)}, u32[]{:S(2)}) copy-start(bf16[24,192,128]{2,1,0:T(8,128)(2,1)} %param.15) | copy-start | bytes 3538948

commit v5 on v4

--- a/solution.py
+++ b/solution.py
@@ -135,17 +135,17 @@
         ))
     load = pltpu.make_async_copy(out_proj, weights, load_sem)
     load.start()
-    for e in range(slots):
-        for copy in unit_loads(jnp.int32(e)):
-            copy.start()
-    for g in range(down_slots):
-        down_load(g).start()
     gathered[me] = attended[...]
     total = dev_count * attended.shape[0]
     rest[...] = residual[...].astype(f32).reshape(rest.shape)
     load.wait()
     for copy in copies:
         copy.wait()
+    for e in range(slots):
+        for copy in unit_loads(jnp.int32(e)):
+            copy.start()
+    for g in range(down_slots):
+        down_load(g).start()
     features = gathered[...].astype(f32).reshape(total, -1).astype(bf16)
     acc[...] = jnp.dot(features, weights[...], preferred_element_type=f32)
     block = rest[t] + sum_over_tp(

time: 70.5 us -> 67.9 us (0.963)
  Pallas kernels: 61.2 us -> 58.6 us
    pallas_call x1, Pallas kernels: 61.2 us -> 58.6 us  [layer(): pl.pallas_call(functools.partial(layer_kernel, dev_count), out_shape=jax....]
where the time goes in v5:
time: 67.9 us; the launch traced here: 67.6 us
  Pallas kernels  58.6 us (86%)
  local copies, waits for them, and re-layouts  4.15 us (6%)
  other arithmetic  2.58 us (4%)
  matrix products  2.23 us (3%)
    pallas_call x1, Pallas kernels, layer(): pl.pallas_call(functools.partial(layer_kernel, dev_count), out_shape=jax....  58.6 us
    unnamed x9, local copies, waits for them, and re-layouts  3.21 us

profile of v5, /device:TPU:0, one launch (start us, length us, event | category | flops | bytes accessed | tf_op | source)
XLA Modules:
  0.0 67.6 jit_solution(13123162215595302104)
XLA Ops:
  0.0 0.0 copy-start
  0.0 0.9 %select_reduce_fusion = f32[8,96]{1,0:T(8,128)S(1)} fusion(f32[96,8]{0,1:T(8,128)} %param.24, s32[96,8]{0,1:T(8,128)} %param.23, s32[8]{0:T(128)S(1)} %iota_add_fusion), kind=kLoop, calls=%fused_computation.10 | loop fusion | flops 17664 | bytes 9248 | tf_op jit(solution)/shard_map/reduce_sum | solution.py:323
  0.9 0.7 %iota_compare_fusion = pred[24,192]{1,0:T(8,128)(4,1)S(1)} fusion(s32[24]{0:T(128)} %param.19), kind=kLoop, calls=%fused_computation.11 | loop fusion | flops 4608 | bytes 4704 | tf_op jit(solution)/shard_map/lt | solution.py:38
  1.6 0.7 %convert_element_type.24 = f32[24,128]{1,0:T(8,128)S(1)} convert(bf16[24,128]{1,0:T(8,128)(2,1)} %param.18) | non-fusion elementwise | flops 3072 | bytes 18432 | tf_op jit(solution)/shard_map/convert_element_type | solution.py:51
  2.3 0.9 %copy.23 = bf16[3,8,16,128]{3,2,1,0:T(8,128)(2,1)S(1)} copy(bf16[3,8,16,128]{3,1,2,0:T(8,128)(2,1)} %bitcast.20) | data formatting | bytes 196608
  3.2 0.0 copy-start.2
  3.2 0.9 %fusion.5 = f32[24,1,16]{2,1,0:T(1,128)S(1)} fusion(bf16[24,16,128]{2,1,0:T(8,128)(2,1)S(1)} %bitcast.18, bf16[24,128,1]{1,0,2:T(8,128)(2,1)} %bitcast.26), kind=kOutput, calls=%fused_computation.12 | convolution fusion | flops 98304 | bytes 105984 | tf_op jit(solution)/shard_map/rkgd,rkd->rkg/dot_general | solution.py:35
  4.2 0.0 copy-done
  4.2 0.8 %fusion.9 = (f32[24,16]{1,0:T(8,128)S(1)}, f32[24,16,192]{2,1,0:T(8,128)S(1)}) fusion(bf16[24,16,128]{2,1,0:T(8,128)(2,1)S(1)} %bitcast.19, bf16[24,192,128]{2,1,0:T(8,128)(2,1)S(1)} %copy-done, pred[24,192]{1,0:T(8,128)(4,1)S(1)} %iota_compare_fusion), kind=kOutput, calls=%fused_computation.20 | convolution fusion | flops 19095168 | bytes 1579008 | tf_op jit(solution)/shard_map/rkgd,rlkd->rkgl/dot_general | solution.py:31
  5.0 0.2 fusion.2
  5.3 0.0 copy-done.2
  5.3 0.5 fusion.1
  5.8 0.7 copy.28
  6.4 0.9 %copy.20.dense = f32[8,96,1]{2,1,0:T(8,128)} copy(f32[8,96,1]{1,0,2:T(8,128)S(1)} %bitcast.25) | data formatting | bytes 6144 | tf_op jit(solution)/shard_map/broadcast_in_dim | solution.py:323
  7.4 0.0 copy-start.1
  7.4 58.6 %shard_map.136 = bf16[96,1024]{1,0:T(8,128)(2,1)} custom-call(bf16[24,2048]{1,0:T(8,128)(2,1)} %bitcast.17, bf16[2048,1024]{1,0:T(8,128)(2,1)} %out_proj.1, bf16[96,1024]{1,0:T(8,128)(2,1)} %residual.1, f32[1,4096]{1,0:T(1,128)} %bitcast.24, f32[8,96,1]{2,1,0:T(8,128)} %copy.20.dense, bf16[8,4096,384]{2,1,0:T(8,128)(2,1)} %gate.1, bf16[8,4096,384]{2,1,0:T(8,128)(2,1)} %up.1, ...), custom_call_target="tpu_custom_call" | custom-call | tf_op jit(solution)/shard_map/pallas_call | solution.py:280
  66.0 1.6 %copy.30 = bf16[96,1024]{1,0:T(8,128)(2,1)} copy(bf16[96,1024]{1,0:T(8,128)(2,1)} %shard_map.136) | data formatting | bytes 393216
  67.6 0.0 copy-done.1
  (3 shorter events, 0.0 us)
Async XLA Ops:
  0.0 4.2 %copy-start = (bf16[24,192,128]{2,1,0:T(8,128)(2,1)S(1)}, bf16[24,192,128]{2,1,0:T(8,128)(2,1)}, u32[]{:S(2)}) copy-start(bf16[24,192,128]{2,1,0:T(8,128)(2,1)} %param.15) | copy-start | bytes 3538948
  3.2 2.0 %copy-start.2 = (bf16[24,192,128]{2,1,0:T(8,128)(2,1)S(1)}, bf16[24,192,128]{2,1,0:T(8,128)(2,1)}, u32[]{:S(2)}) copy-start(bf16[24,192,128]{2,1,0:T(8,128)(2,1)} %param.16) | copy-start | bytes 3538948
  7.4 60.2 %copy-start.1 = (bf16[24,192,128]{2,1,0:T(8,128)(2,1)S(1)}, bf16[24,192,128]{2,1,0:T(8,128)(2,1)}, u32[]{:S(2)}) copy-start(bf16[24,192,128]{2,1,0:T(8,128)(2,1)} %param.15) | copy-start | bytes 3538948
